TPU v7x, 32 devices: a whole 2x2x4 slice. The times are simulated.
32 devices in a mesh: expert: 8 (over z, x), replica: 4 (over y, core).
Axes of the slice: x: 2, y: 2, z: 4, core: 2. Of those that a mesh axis runs over, the one named last changes fastest.
Arguments:
- x_tokens: bfloat16 [4096, 2048], P(('expert', 'replica')), may hold values from -6 to 6
- d_out: bfloat16 [4096, 2048], P(('expert', 'replica')), may hold values from -3 to 3
- expert_ids: int32 [4096, 2], P(('expert', 'replica')), may hold values from 0 to 7, all different within a row; in each aligned block of 128 rows (0 to 127, 128 to 255, ...) at most 64 rows name the same one
- combine: float32 [4096, 2], P(('expert', 'replica')), may hold values from 0.1 to 1
- w_stack: bfloat16 [8, 1408, 6144], P('expert'), may hold values from -0.125 to 0.125
Outputs:
- d_tokens: bfloat16 [4096, 2048], P(('expert', 'replica'))
- g_stack: bfloat16 [8, 1408, 6144], P('expert', 'replica')
Inputs may be any that keep to these rules, and one draw needn't show every extreme that they name: `expert_ids`: in the tokens of one device (aligned blocks of 128 tokens) each expert is named by at most 64 routes, and by exactly 64 in some block; a token's 2 experts differ.
All inputs are finite; a program needn't handle non-finite values.
Results may differ from a plain program's by a relative error of at most 0.013.
Values may be sent and summed in bfloat16 or wider, within the bound.
No kernel may reach another device: no remote copies, remote signals or barrier semaphores. Data moves between devices by JAX's collectives and lax.ppermute only.
A program may use at most 128 MiB of HBM per device.

v0:
```python
import functools

import jax
import jax.numpy as jnp
from jax import lax
from jax.experimental import pallas as pl
from jax.experimental.pallas import tpu as pltpu
from jax.sharding import PartitionSpec as P

BF16 = jnp.bfloat16
F32 = jnp.float32
RING = (0, 1, 3, 2)
VMEM_LIMIT = 44 * 1024 * 1024


def params():
    return pltpu.CompilerParams(vmem_limit_bytes=VMEM_LIMIT)


def smem():
    return pl.BlockSpec(memory_space=pltpu.SMEM)


def anywhere():
    return pl.BlockSpec(memory_space=pl.ANY)


def inside():
    return pl.BlockSpec(memory_space=pltpu.VMEM)


def small_cost():
    return pl.CostEstimate(flops=1024, bytes_accessed=1024, transcendentals=0)


def tile_of(width, most):
    return most if width % most == 0 else width


class Order:
    def __init__(self):
        self.last = []

    def call(self, kernel, specs, operands, deps=(), cost=None, **options):
        extra = list(deps) + self.last
        count = len(operands)

        def body_of(*refs):
            kernel(*refs[:count], *refs[count + len(extra) :])

        outs = pl.pallas_call(
            body_of,
            in_specs=list(specs) + [anywhere()] * len(extra),
            compiler_params=params(),
            cost_estimate=cost or small_cost(),
            **options,
        )(*operands, *extra)
        self.last = [outs[-1] if isinstance(outs, (list, tuple)) else outs]
        return outs


def placing_of(base, own, meta, expert_count, capacity):
    tokens = meta.shape[1]
    id_first, id_second = meta[0:1, :], meta[1:2, :]
    scale_first, scale_second = meta[2:3, :], meta[3:4, :]
    row = lax.broadcasted_iota(jnp.int32, (max(16, expert_count), tokens), 0)
    expert = (base + jnp.bitwise_xor(row, own)).astype(F32)
    first = id_first == expert
    member = jnp.where(first | (id_second == expert), 1.0, 0.0)
    scale = jnp.where(first, scale_first, scale_second)
    earlier = lax.broadcasted_iota(jnp.int32, (tokens, tokens), 0)
    later = lax.broadcasted_iota(jnp.int32, (tokens, tokens), 1)
    before = jnp.where(earlier < later, 1.0, 0.0).astype(BF16)
    rank = jnp.dot(member.astype(BF16), before, preferred_element_type=F32)
    rank = jnp.where(member > 0.0, rank, -1.0)
    slot = lax.broadcasted_iota(jnp.int32, (capacity, tokens), 0).astype(F32)
    hits, scales = [], []
    for d in range(expert_count):
        hit = jnp.where(rank[d : d + 1, :] == slot, 1.0, 0.0)
        hits.append(hit)
        scales.append(jnp.sum(hit * scale[d : d + 1, :], axis=1, keepdims=True))
    return jnp.concatenate(hits, axis=0), jnp.concatenate(scales, axis=0)


def rounded(value):
    return value.astype(BF16).astype(F32)


def meta_columns(meta):
    scale = meta[2:4, :]
    top = rounded(scale)
    middle = rounded(scale - top)
    rest = scale - top - middle
    filler = jnp.zeros((120, meta.shape[1]), F32)
    return jnp.concatenate([meta[0:2, :], top, middle, rest, filler], axis=0).T.astype(BF16)


def meta_rows(columns):
    rows = columns.astype(F32).T
    scale = rows[2:4, :] + rows[4:6, :] + rows[6:8, :]
    return jnp.concatenate([rows[0:2, :], scale], axis=0)


def first_kernel(columns, capacity, place_ref, meta_ref, x_ref, *refs):
    x_out, keep_ref, send_refs = refs[0], refs[1], refs[2 : columns + 1]
    scales_ref, hits_ref = refs[columns + 1 :]
    width = x_ref.shape[1]
    meta = meta_ref[...]
    x = x_ref[...]
    x_out[:, :width] = x
    x_out[:, width:] = meta_columns(meta)
    hits, scales = placing_of(place_ref[0], place_ref[1], meta, columns, capacity)
    hits = hits.astype(BF16)
    hits_ref[...] = hits
    scales_ref[...] = jnp.broadcast_to(scales, scales_ref.shape)
    picked = jnp.dot(hits, x, preferred_element_type=F32).astype(BF16)
    keep_ref[...] = picked[:capacity, :]
    for d in range(1, columns):
        send_refs[d - 1][...] = picked[d * capacity : (d + 1) * capacity, :]


def select_first(order, place, meta, x, columns, capacity):
    tokens, width = x.shape
    count = columns * capacity
    outs = order.call(
        functools.partial(first_kernel, columns, capacity),
        [smem(), inside(), inside()],
        [place, meta, x],
        out_specs=[inside()] * (columns + 3),
        out_shape=[jax.ShapeDtypeStruct((tokens, width + 128), BF16)]
        + [jax.ShapeDtypeStruct((capacity, width), BF16)] * columns
        + [
            jax.ShapeDtypeStruct((count, 128), F32),
            jax.ShapeDtypeStruct((count, tokens), BF16),
        ],
        name="select_first",
    )
    return outs[0], outs[1:-2], outs[-2], outs[-1]


def both_kernel(columns, capacity, again, place_ref, x_ref, old_scales, old_hits, d_ref, *refs):
    keep_x, keep_d, refs = refs[0], refs[1], refs[2:]
    pair_refs, send_refs, refs = refs[: columns - 1], refs[columns - 1 : 2 * columns - 2], refs[2 * columns - 2 :]
    scales_ref, hits_ref = refs[-2:]
    width = d_ref.shape[1]
    rows = d_ref[...]
    if again:
        refs[0][...] = rows
    meta = meta_rows(x_ref[:, width:])
    hits, scales = placing_of(place_ref[0], place_ref[1], meta, columns, capacity)
    hits = hits.astype(BF16)
    hits_ref[...] = hits
    scales_ref[...] = jnp.broadcast_to(scales, scales_ref.shape)
    x = jnp.dot(hits, x_ref[:, :width], preferred_element_type=F32).astype(BF16)
    dy = jnp.dot(old_hits[...], rows, preferred_element_type=F32)
    dy = (dy * old_scales[:, 0:1]).astype(BF16)
    keep_x[...] = x[:capacity, :]
    keep_d[...] = dy[:capacity, :]
    for d in range(1, columns):
        part = slice(d * capacity, (d + 1) * capacity)
        pair_refs[d - 1][0] = x[part, :]
        pair_refs[d - 1][1] = dy[part, :]
        send_refs[d - 1][...] = x[part, :]


def select_both(order, place, x, scales, hits, d_rows, columns, again, deps):
    tokens, width = d_rows.shape
    count = hits.shape[0]
    capacity = count // columns
    shapes = [(capacity, width)] * 2
    shapes += [(2, capacity, width)] * (columns - 1) + [(capacity, width)] * (columns - 1)
    shapes += [(tokens, width)] * again
    outs = order.call(
        functools.partial(both_kernel, columns, capacity, again),
        [smem()] + [inside()] * 4,
        [place, x, scales, hits, d_rows],
        deps,
        out_specs=[inside()] * (len(shapes) + 2),
        out_shape=[jax.ShapeDtypeStruct(shape, BF16) for shape in shapes]
        + [
            jax.ShapeDtypeStruct((count, 128), F32),
            jax.ShapeDtypeStruct((count, tokens), BF16),
        ],
        name="select_both",
    )
    pairs, sends = outs[2 : columns + 1], outs[columns + 1 : 2 * columns]
    return outs[0], outs[1], pairs, sends, outs[-3], outs[-2], outs[-1]


def last_kernel(columns, scales_ref, hits_ref, d_ref, *out_refs):
    capacity = out_refs[0].shape[0]
    picked = jnp.dot(hits_ref[...], d_ref[...], preferred_element_type=F32)
    picked = (picked * scales_ref[:, 0:1]).astype(BF16)
    for d in range(columns):
        out_refs[d][...] = picked[d * capacity : (d + 1) * capacity, :]


def select_last(order, scales, hits, d_rows, columns, deps):
    width = d_rows.shape[1]
    capacity = hits.shape[0] // columns
    return order.call(
        functools.partial(last_kernel, columns),
        [inside()] * 3,
        [scales, hits, d_rows],
        deps,
        out_specs=[inside()] * columns,
        out_shape=[jax.ShapeDtypeStruct((capacity, width), BF16)] * columns,
        name="select_last",
    )


def place_all_kernel(experts, capacity, meta_ref, hits_ref):
    hits, _ = placing_of(0, 0, meta_ref[...], experts, capacity)
    hits_ref[...] = hits.astype(BF16)


def place_all(order, meta, experts, capacity):
    return order.call(
        functools.partial(place_all_kernel, experts, capacity),
        [inside()],
        [meta],
        out_specs=inside(),
        out_shape=jax.ShapeDtypeStruct((experts * capacity, meta.shape[1]), BF16),
        name="place_all",
    )


def merge_kernel(hits_ref, slots_ref, out_ref):
    out_ref[...] = lax.dot_general(
        hits_ref[...], slots_ref[...], (((0,), (0,)), ((), ())), preferred_element_type=F32
    ).astype(BF16)


def merge(order, hits, slots):
    return order.call(
        merge_kernel,
        [inside(), inside()],
        [hits, slots],
        out_shape=jax.ShapeDtypeStruct((hits.shape[1], slots.shape[1]), BF16),
        out_specs=inside(),
        name="merge",
    )


def start_rows(refs, target, sems):
    capacity = target.shape[0] // len(refs)
    copies = []
    for i, (ref, which) in enumerate(refs):
        source = ref if which is None else ref.at[which]
        rows = target.at[pl.ds(i * capacity, capacity)]
        copies.append(pltpu.make_async_copy(source, rows, sems.at[i]))
    for copy in copies:
        copy.start()
    return copies


def split_pieces(pieces):
    return [array for array, _ in pieces], [which for _, which in pieces]


def start_weights(w_ref, units, part, target, sem):
    width = target.shape[-1]
    copy = pltpu.make_async_copy(w_ref.at[0, units, pl.ds(part * width, width)], target, sem)
    copy.start()
    return copy


def gate_up_kernel(whiches, *refs):
    count = len(whiches)
    x_refs, w_ref, refs = refs[:count], refs[count], refs[count + 1 :]
    hid_ref, act_ref, slope_ref, x_all, x_turned, w_pair, sems, w_sems = refs
    half = hid_ref.shape[1]
    rows = start_rows(list(zip(x_refs, whiches)), x_all, sems)
    weights = []
    for t in range(2):
        for k in range(2):
            units = pl.ds(t * half, half)
            weights.append(start_weights(w_ref, units, k, w_pair.at[t, k], w_sems.at[2 * t + k]))
    for copy in rows:
        copy.wait()
    x_turned[...] = x_all[...].T
    for t in range(2):
        weights[2 * t].wait()
        gate = jnp.dot(w_pair[t, 0], x_turned[...], preferred_element_type=F32)
        weights[2 * t + 1].wait()
        up = jnp.dot(w_pair[t, 1], x_turned[...], preferred_element_type=F32)
        sig = jax.nn.sigmoid(gate)
        act = gate * sig
        hid_ref[t] = (act * up).astype(BF16)
        act_ref[t] = act
        slope_ref[t] = up * sig * (1.0 + gate * (1.0 - sig))


def gate_up(order, pieces, w_stack, capacity, deps=()):
    arrays, whiches = split_pieces(pieces)
    width = arrays[0].shape[-1]
    rows, hidden = len(pieces) * capacity, w_stack.shape[1]
    return order.call(
        functools.partial(gate_up_kernel, whiches),
        [anywhere()] * (len(pieces) + 1),
        [*arrays, w_stack],
        deps,
        out_specs=[inside()] * 3,
        out_shape=[
            jax.ShapeDtypeStruct((2, hidden // 2, rows), BF16),
            jax.ShapeDtypeStruct((2, hidden // 2, rows), F32),
            jax.ShapeDtypeStruct((2, hidden // 2, rows), F32),
        ],
        scratch_shapes=[
            pltpu.VMEM((rows, width), BF16),
            pltpu.VMEM((width, rows), BF16),
            pltpu.VMEM((2, 2, hidden // 2, width), BF16),
            pltpu.SemaphoreType.DMA((len(pieces),)),
            pltpu.SemaphoreType.DMA((4,)),
        ],
        name="gate_up",
    )


def backward_kernel(whiches, columns, first_step, place_ref, *refs):
    count = len(whiches)
    dy_refs, (act_ref, slope_ref, w_ref), refs = refs[:count], refs[count : count + 3], refs[count + 3 :]
    dx_ref, send_ref, keep_ref, dy_all, dy_turned, total, w_all, sems, w_sems, out_sems = refs[-10:]
    half = act_ref.shape[1]
    capacity = dx_ref.shape[1]
    rows = start_rows(list(zip(dy_refs, whiches)), dy_all, sems)
    halves = [jnp.bitwise_xor(place_ref[2], 1 - t) for t in range(2)]
    weights = []
    for t, which in enumerate(halves):
        units = pl.ds(pl.multiple_of(which * half, half), half)
        for k in (2, 0, 1):
            weights.append(start_weights(w_ref, units, k, w_all.at[t, k], w_sems.at[3 * t + k]))
    for copy in rows:
        copy.wait()
    dy_turned[...] = dy_all[...].T
    sums = None
    for t, which in enumerate(halves):
        weights[3 * t].wait()
        d_hidden = jnp.dot(w_all[t, 2], dy_turned[...], preferred_element_type=F32)
        d_up = (d_hidden * act_ref[which]).astype(BF16)
        d_gate = (d_hidden * slope_ref[which]).astype(BF16)
        out_ref = (send_ref, keep_ref)[t]
        out_ref[:half, :] = d_gate
        out_ref[half:, :] = d_up
        for k, factor in enumerate((d_gate, d_up)):
            weights[3 * t + 1 + k].wait()
            part = jnp.dot(factor.T, w_all[t, k], preferred_element_type=F32)
            sums = part if sums is None else sums + part
    total[...] = sums.astype(BF16)
    copies = []
    for i in range(count):
        block = place_ref[4 + first_step + i // columns] + jnp.bitwise_xor(
            place_ref[1], i % columns
        )
        copies.append(
            pltpu.make_async_copy(
                total.at[pl.ds(i * capacity, capacity)], dx_ref.at[block], out_sems.at[i]
            )
        )
    for copy in copies:
        copy.start()
    for copy in copies:
        copy.wait()


def backward(order, place, pieces, act, slope, w_stack, columns, first_step, dx, shape, deps):
    arrays, whiches = split_pieces(pieces)
    count = len(pieces)
    capacity, width = shape[1:]
    rows, hidden = count * capacity, w_stack.shape[1]
    operands = [place, *arrays, act, slope, w_stack]
    specs = [smem()] + [anywhere()] * count + [inside()] * 2 + [anywhere()]
    aliases = {}
    if dx is not None:
        aliases = {len(operands): 0}
        operands.append(dx)
        specs.append(anywhere())
    return order.call(
        functools.partial(backward_kernel, whiches, columns, first_step),
        specs,
        operands,
        deps,
        out_specs=[anywhere(), inside(), inside()],
        out_shape=[jax.ShapeDtypeStruct(shape, BF16)]
        + [jax.ShapeDtypeStruct((hidden, rows), BF16)] * 2,
        scratch_shapes=[
            pltpu.VMEM((rows, width), BF16),
            pltpu.VMEM((width, rows), BF16),
            pltpu.VMEM((rows, width), BF16),
            pltpu.VMEM((2, 3, hidden // 2, width), BF16),
            pltpu.SemaphoreType.DMA((count,)),
            pltpu.SemaphoreType.DMA((6,)),
            pltpu.SemaphoreType.DMA((count,)),
        ],
        input_output_aliases=aliases,
        name="backward",
    )


def side_by_side(refs, whiches, columns):
    return jnp.concatenate(
        [
            ref[:, columns] if which is None else ref[which, :, columns]
            for ref, which in zip(refs, whiches)
        ],
        axis=0,
    )


def grad_x_kernel(act_count, whiches, place_ref, *refs):
    acts, rows = refs[:act_count], refs[act_count:-2]
    send_ref, keep_ref = refs[-2:]
    own, width = send_ref.shape[1:]
    low = place_ref[3]
    lefts = []
    for who in (1 - low, low):
        for lead in range(2):
            start = pl.multiple_of((2 * lead + who) * own, own)
            lefts.append(jnp.concatenate([ref[pl.ds(start, own), :] for ref in acts], axis=1))
    left = jnp.concatenate(lefts, axis=0)
    tile = tile_of(width, 512)
    for n in range(0, width, tile):
        columns = slice(n, n + tile)
        right = side_by_side(rows, whiches, columns)
        total = jnp.dot(left, right, preferred_element_type=F32).astype(BF16)
        for lead in range(2):
            send_ref[lead, :, columns] = total[lead * own : (lead + 1) * own]
            keep_ref[lead, :, columns] = total[(2 + lead) * own : (3 + lead) * own]


def grad_x(order, place, acts, rows, width, deps):
    own = acts[0].shape[0] // 4
    arrays, whiches = split_pieces(rows)
    return order.call(
        functools.partial(grad_x_kernel, len(acts), whiches),
        [smem()] + [inside()] * (len(acts) + len(rows)),
        [place, *acts, *arrays],
        deps,
        out_specs=[inside()] * 2,
        out_shape=[jax.ShapeDtypeStruct((2, own, width), BF16)] * 2,
        name="grad_x",
    )


def grad_down_kernel(hid_count, whiches, place_ref, *refs):
    hids, rows, out_refs = refs[:hid_count], refs[hid_count:-4], refs[-4:]
    own, width = out_refs[0].shape
    high, low = place_ref[2], place_ref[3]
    lefts = []
    for lead in (1 - high, high):
        for who in (1 - low, low):
            start = pl.multiple_of(who * own, own)
            lefts.append(
                jnp.concatenate([ref[lead, pl.ds(start, own), :] for ref in hids], axis=1)
            )
    left = jnp.concatenate(lefts, axis=0)
    tile = tile_of(width, 512)
    for n in range(0, width, tile):
        columns = slice(n, n + tile)
        right = side_by_side(rows, whiches, columns)
        total = jnp.dot(left, right, preferred_element_type=F32).astype(BF16)
        for i in range(4):
            out_refs[i][:, columns] = total[i * own : (i + 1) * own]


def grad_down(order, place, hids, rows, width, deps):
    own = hids[0].shape[1] // 2
    arrays, whiches = split_pieces(rows)
    return order.call(
        functools.partial(grad_down_kernel, len(hids), whiches),
        [smem()] + [inside()] * (len(hids) + len(rows)),
        [place, *hids, *arrays],
        deps,
        out_specs=[inside()] * 4,
        out_shape=[jax.ShapeDtypeStruct((own, width), BF16)] * 4,
        name="grad_down",
    )


def sum_kernel(down_count, keep_ref, come_ref, *refs):
    downs, out_ref = refs[:down_count], refs[down_count]
    width = keep_ref.shape[2]
    for lead in range(2):
        total = keep_ref[lead].astype(F32) + come_ref[lead].astype(F32)
        out_ref[:, lead * width : (lead + 1) * width] = total.astype(BF16)
    total = downs[0][...].astype(F32)
    for ref in downs[1:]:
        total = total + ref[...].astype(F32)
    out_ref[:, 2 * width :] = total.astype(BF16)


def sum_all(order, keep, come, downs):
    _, own, width = keep.shape
    return order.call(
        functools.partial(sum_kernel, len(downs)),
        [inside()] * (2 + len(downs)),
        [keep, come, *downs],
        cost=pl.CostEstimate(flops=1024, bytes_accessed=1 << 26, transcendentals=0),
        out_specs=inside(),
        out_shape=jax.ShapeDtypeStruct((own, 3 * width), BF16),
        name="sum_all",
    )


def body(x_tokens, d_out, expert_ids, combine, w_stack):
    tokens, width = x_tokens.shape
    experts = lax.axis_size("expert")
    replicas = lax.axis_size("replica")
    planes = len(RING)
    columns = experts // planes
    capacity = 2 * tokens * expert_ids.shape[1] // experts

    position = lax.axis_index("expert")
    replica = lax.axis_index("replica")
    plane, column = position // columns, position % columns
    high, low = replica // 2, replica % 2
    ring_place = plane ^ (plane >> 1)
    sources = [(ring_place - s) & (planes - 1) for s in range(planes)]
    firsts = [(source ^ (source >> 1)) * columns for source in sources]
    place = jnp.stack([plane * columns, column, high, low, *firsts]).astype(jnp.int32)

    def along_ring(value):
        pairs = [
            (RING[i] * columns + c, RING[(i + 1) % planes] * columns + c)
            for i in range(planes)
            for c in range(columns)
        ]
        return lax.ppermute(value, "expert", pairs)

    def across(value, d, r):
        pairs = [
            ((p * columns + c) * replicas + k, (p * columns + (c ^ d)) * replicas + (k ^ r))
            for p in range(planes)
            for c in range(columns)
            for k in range(replicas)
        ]
        return lax.ppermute(value, ("expert", "replica"), pairs)

    def exchange(values, r):
        return [across(value, d + 1, r) for d, value in enumerate(values)]

    order = Order()
    meta = jnp.concatenate([expert_ids.T.astype(F32), combine.T], axis=0)

    x_0, picked, scales, hits = select_first(order, place, meta, x_tokens, columns, capacity)
    x_1 = along_ring(x_0)
    x_pieces = [(picked[0], None)] + [(value, None) for value in exchange(picked[1:], 0)]
    x_other = [(across(picked[0], 0, 2), None)] + [(v, None) for v in exchange(picked[1:], 2)]
    dy_pieces = []
    all_hits = place_all(order, meta, experts, capacity)
    x_block, d_block = x_1, d_out
    hids, acts_kept, acts_come = [], [], []
    dx = None
    dx_shape = (experts, capacity, width)
    factors = None
    for s in range(1, planes):
        x_next = along_ring(x_block) if s < planes - 1 else None
        waits = {
            1: [value for value, _ in x_pieces[1:] + x_other],
            2: [value for value, _ in x_other[columns:]],
            3: [],
        }[s]
        d_next = along_ring(d_block) if s > 1 else None
        keep_x, keep_d, pairs, sends, again, scales, hits = select_both(
            order, place, x_block, scales, hits, d_block, columns, s == 1, waits
        )
        if s == 1:
            d_next = along_ring(again)
        come = exchange(pairs, 0)
        x_pieces += [(keep_x, None)] + [(value, 0) for value in come]
        dy_pieces += [(keep_d, None)] + [(value, 1) for value in come]
        x_other += [(across(keep_x, 0, 2), None)] + [(v, None) for v in exchange(sends, 2)]
        x_block, d_block = x_next, d_next
        if s == 1:
            hid, *factors = gate_up(order, x_pieces[: 2 * columns], w_stack, capacity)
            hids.append(hid)
        if s == 2:
            dx, send, keep = backward(
                order, place, dy_pieces[: 2 * columns], *factors, w_stack, columns, 0, None,
                dx_shape, [value for value, _ in x_other[2 * columns : 3 * columns]],
            )
            acts_kept.append(keep)
            acts_come.append(across(send, 0, 2))
    picked = select_last(order, scales, hits, d_block, columns, [])
    dy_pieces += [(picked[0], None)] + [(value, None) for value in exchange(picked[1:], 0)]
    hid, *factors = gate_up(order, x_pieces[2 * columns :], w_stack, capacity)
    hids.append(hid)
    send_other, keep_other, send_own, down_own = grad_down(
        order, place, hids, dy_pieces, width,
        [acts_come[0]] + [value for value, _ in x_other[3 * columns :]],
    )
    dx, send, keep = backward(
        order, place, dy_pieces[2 * columns :], *factors, w_stack, columns, 2, dx, dx_shape, [],
    )
    acts_kept.append(keep)
    acts_come.append(across(send, 0, 2))
    returned = lax.all_to_all(dx, "expert", split_axis=0, concat_axis=0, tiled=True)
    summed = keep_other.astype(F32) + across(send_other, 0, 1).astype(F32)
    summed = summed.astype(BF16)
    down_y = across(summed, 0, 2)
    down_core = across(send_own, 0, 1)

    send, keep = grad_x(
        order, place, acts_kept + acts_come, x_pieces + x_other, width, [summed, down_core]
    )
    g_rows = sum_all(order, keep, across(send, 0, 1), [down_own, down_core, down_y])
    d_tokens = merge(order, all_hits, returned.reshape(experts * capacity, width))
    return d_tokens, g_rows[None]


def solution(mesh):
    return jax.shard_map(
        body,
        mesh=mesh,
        in_specs=(
            P(("expert", "replica"), None),
            P(("expert", "replica"), None),
            P(("expert", "replica"), None),
            P(("expert", "replica"), None),
            P("expert", None, None),
        ),
        out_specs=(P(("expert", "replica"), None), P("expert", "replica", None)),
        check_vma=False,
    )
```

profile of v0, /device:TPU:0, one launch (start us, length us, event | category | flops | bytes accessed | tf_op | source)
XLA Modules:
  0.0 212.2 jit_solution(16885021623641382010)
XLA Ops:
  4.1 3.1 %collective-permute-start = (bf16[128,2176]{1,0:T(8,128)(2,1)S(1)}, bf16[128,2176]{1,0:T(8,128)(2,1)S(1)}, u32[]{:S(2)}, u32[]{:S(2)}) collective-permute-start(bf16[128,2176]{1,0:T(8,128)(2,1)S(1)} %get-tuple-element.47), channel_id=1, source_target_pairs={{0,8},{4,12},{8,24},{12,28},{24,16},{28,20},{16,0},{20,4},{1,9},{5... | collective-permute-start | bytes 1671176 | tf_op jit(solution)/shard_map/ppermute | solution.py:528
  10.9 5.6 %collective-permute-done.3.refs_5_.refs_1_.refs_6_ = bf16[64,2048]{1,0:T(8,128)(2,1)S(1)} collective-permute-done((bf16[64,2048]{1,0:T(8,128)(2,1)S(1)}, bf16[64,2048]{1,0:T(8,128)(2,1)S(1)}, u32[]{:S(2)}, u32[]{:S(2)}) %collective-permute-start.3) | collective-permute-done | bytes 262176 | tf_op jit(solution)/shard_map/ppermute | solution.py:537
  16.4 5.4 %collective-permute-done.4.refs_6_.refs_13_ = bf16[64,2048]{1,0:T(8,128)(2,1)S(1)} collective-permute-done((bf16[64,2048]{1,0:T(8,128)(2,1)S(1)}, bf16[64,2048]{1,0:T(8,128)(2,1)S(1)}, u32[]{:S(2)}, u32[]{:S(2)}) %collective-permute-start.4) | collective-permute-done | bytes 262176 | tf_op jit(solution)/shard_map/ppermute | solution.py:537
  24.2 2.6 %collective-permute-start.6 = (bf16[128,2048]{1,0:T(8,128)(2,1)S(1)}, bf16[128,2048]{1,0:T(8,128)(2,1)S(1)}, u32[]{:S(2)}, u32[]{:S(2)}) collective-permute-start(bf16[128,2048]{1,0:T(8,128)(2,1)S(1)} %get-tuple-element.53), channel_id=1, source_target_pairs={{0,8},{4,12},{8,24},{12,28},{24,16},{28,20},{16,0},{20,4},{1,9},{5... | collective-permute-start | bytes 1572872 | tf_op jit(solution)/shard_map/ppermute | solution.py:528
  30.8 9.2 %collective-permute-done.6.refs_4_ = bf16[128,2048]{1,0:T(8,128)(2,1)S(1)} collective-permute-done((bf16[128,2048]{1,0:T(8,128)(2,1)S(1)}, bf16[128,2048]{1,0:T(8,128)(2,1)S(1)}, u32[]{:S(2)}, u32[]{:S(2)}) %collective-permute-start.6) | collective-permute-done | bytes 524320 | tf_op jit(solution)/shard_map/ppermute | solution.py:528
  42.2 8.6 %gate_up.2 = (bf16[2,704,256]{2,1,0:T(8,128)(2,1)S(1)}, f32[2,704,256]{2,1,0:T(8,128)S(1)}, f32[2,704,256]{2,1,0:T(8,128)S(1)}) custom-call(bf16[64,2048]{1,0:T(8,128)(2,1)S(1)} %get-tuple-element.50.refs_0_.refs_5_, bf16[64,2048]{1,0:T(8,128)(2,1)S(1)} %collective-permute-done.3.refs_5_.refs_1_.refs_6_, ...), custom_call_target="tpu_custom_call" | custom-call | flops 1024 | bytes 1024 | tf_op jit(solution)/shard_map/gate_up/pallas_call | solution.py:51
  58.4 4.8 %collective-permute-done.10.refs_4_ = bf16[128,2048]{1,0:T(8,128)(2,1)S(1)} collective-permute-done((bf16[128,2048]{1,0:T(8,128)(2,1)S(1)}, bf16[128,2048]{1,0:T(8,128)(2,1)S(1)}, u32[]{:S(2)}, u32[]{:S(2)}) %collective-permute-start.10) | collective-permute-done | bytes 524320 | tf_op jit(solution)/shard_map/ppermute | solution.py:528
  63.2 1.7 collective-permute-start.15
  64.9 3.2 %collective-permute-done.13.refs_9_.refs_18_ = bf16[64,2048]{1,0:T(8,128)(2,1)S(1)} collective-permute-done((bf16[64,2048]{1,0:T(8,128)(2,1)S(1)}, bf16[64,2048]{1,0:T(8,128)(2,1)S(1)}, u32[]{:S(2)}, u32[]{:S(2)}) %collective-permute-start.13) | collective-permute-done | bytes 262176 | tf_op jit(solution)/shard_map/ppermute | solution.py:537
  68.1 11.6 %backward.2 = (bf16[8,64,2048]{2,1,0:T(8,128)(2,1)S(1)}, bf16[1408,256]{1,0:T(8,128)(2,1)S(1)}, bf16[1408,256]{1,0:T(8,128)(2,1)S(1)}) custom-call(s32[8]{0:T(128)S(1)} %stack.35.refs_0_, bf16[64,2048]{1,0:T(8,128)(2,1)S(1)} %get-tuple-element.60.refs_1_.refs_3_, bf16[2,64,2048]{2,1,0:T(8,128)(2,1)S(1)} %collective-permute-done.9.refs_3_.refs_2_.refs_4_.refs_8_, ...), custom_call_target="tpu_custom_call" | custom-call | flops 1024 | bytes 1024 | tf_op jit(solution)/shard_map/backward/pallas_call | solution.py:51
  81.7 1.8 collective-permute-start.14
  85.6 1.8 collective-permute-start.16
  87.4 8.0 %collective-permute-done.14.refs_3_.refs_8_.refs_2_.refs_12_ = bf16[2,64,2048]{2,1,0:T(8,128)(2,1)S(1)} collective-permute-done((bf16[2,64,2048]{2,1,0:T(8,128)(2,1)S(1)}, bf16[2,64,2048]{2,1,0:T(8,128)(2,1)S(1)}, u32[]{:S(2)}, u32[]{:S(2)}) %collective-permute-start.14) | collective-permute-done | bytes 524320 | tf_op jit(solution)/shard_map/ppermute | solution.py:537
  95.4 8.8 %gate_up.3 = (bf16[2,704,256]{2,1,0:T(8,128)(2,1)S(1)}, f32[2,704,256]{2,1,0:T(8,128)S(1)}, f32[2,704,256]{2,1,0:T(8,128)S(1)}) custom-call(bf16[64,2048]{1,0:T(8,128)(2,1)S(1)} %get-tuple-element.64.refs_0_.refs_9_, bf16[2,64,2048]{2,1,0:T(8,128)(2,1)S(1)} %collective-permute-done.11.refs_4_.refs_1_.refs_6_.refs_10_, ...), custom_call_target="tpu_custom_call" | custom-call | flops 1024 | bytes 1024 | tf_op jit(solution)/shard_map/gate_up/pallas_call | solution.py:51
  105.4 5.5 %grad_down.1 = (bf16[352,2048]{1,0:T(8,128)(2,1)}, bf16[352,2048]{1,0:T(8,128)(2,1)S(1)}, bf16[352,2048]{1,0:T(8,128)(2,1)}, bf16[352,2048]{1,0:T(8,128)(2,1)}) custom-call(s32[8]{0:T(128)S(1)} %stack.35.refs_0_, bf16[2,704,256]{2,1,0:T(8,128)(2,1)S(1)} %get-tuple-element.77.refs_1_, bf16[2,704,256]{2,1,0:T(8,128)(2,1)S(1)} %get-tuple-element.78.refs_2_, ...), custom_call_target="tpu_custom_call" | custom-call | flops 1024 | bytes 1024 | tf_op jit(solution)/shard_map/grad_down/pallas_call | solution.py:51
  113.9 11.9 %backward.3 = (bf16[8,64,2048]{2,1,0:T(8,128)(2,1)S(1)}, bf16[1408,256]{1,0:T(8,128)(2,1)S(1)}, bf16[1408,256]{1,0:T(8,128)(2,1)S(1)}) custom-call(s32[8]{0:T(128)S(1)} %stack.35.refs_0_, bf16[64,2048]{1,0:T(8,128)(2,1)S(1)} %get-tuple-element.67.refs_7_.refs_1_, ...), custom_call_target="tpu_custom_call", output_to_operand_aliasing={{0}: (8, {})} | custom-call | flops 1024 | bytes 1024 | tf_op jit(solution)/shard_map/backward/pallas_call | solution.py:51
  128.8 6.5 %all-to-all-start = ((bf16[8,64,2048]{2,1,0:T(8,128)(2,1)}), bf16[8,64,2048]{2,1,0:T(8,128)(2,1)S(1)}, u32[]{:S(2)}, u32[]{:S(2)}) async-start(bf16[8,64,2048]{2,1,0:T(8,128)(2,1)} %copy-done.4), calls=%async_computation | async-start | bytes 4194304 | tf_op jit(solution)/shard_map/all_to_all | solution.py:597
  137.0 2.5 %add_convert_fusion.refs_21_ = bf16[352,2048]{1,0:T(8,128)(2,1)S(1)} fusion(bf16[352,2048]{1,0:T(8,128)(2,1)} %collective-permute-done.21, bf16[352,2048]{1,0:T(8,128)(2,1)} %copy-done.15), kind=kLoop, calls=%fused_computation | loop fusion | flops 2883584 | bytes 4325376 | tf_op jit(solution)/shard_map/convert_element_type | solution.py:599
  139.5 13.8 %collective-permute-done.20.refs_4_ = bf16[1408,256]{1,0:T(8,128)(2,1)S(1)} collective-permute-done((bf16[1408,256]{1,0:T(8,128)(2,1)}, bf16[1408,256]{1,0:T(8,128)(2,1)S(1)}, u32[]{:S(2)}, u32[]{:S(2)}) %collective-permute-start.20) | collective-permute-done | bytes 720928 | tf_op jit(solution)/shard_map/ppermute | solution.py:537
  159.1 9.0 %grad_x.1 = (bf16[2,352,2048]{2,1,0:T(8,128)(2,1)}, bf16[2,352,2048]{2,1,0:T(8,128)(2,1)}) custom-call(s32[8]{0:T(128)S(1)} %stack.35.refs_0_, bf16[1408,256]{1,0:T(8,128)(2,1)S(1)} %copy-done.10, bf16[1408,256]{1,0:T(8,128)(2,1)S(1)} %copy-done.14, bf16[1408,256]{1,0:T(8,128)(2,1)S(1)} %copy-done.12, bf16[1408,256]{1,0:T(8,128)(2,1)S(1)} %collective-permute-done.20.refs_4_, ...), custom_call_target="tpu_custom_call" | custom-call | flops 1024 | bytes 1024 | tf_op jit(solution)/shard_map/grad_x/pallas_call | solution.py:51
  169.7 32.5 %collective-permute-done.24.refs_4_ = bf16[352,2048]{1,0:T(8,128)(2,1)S(1)} collective-permute-done((bf16[352,2048]{1,0:T(8,128)(2,1)S(1)}, bf16[352,2048]{1,0:T(8,128)(2,1)S(1)}, u32[]{:S(2)}, u32[]{:S(2)}) %collective-permute-start.24) | collective-permute-done | bytes 1441824 | tf_op jit(solution)/shard_map/ppermute | solution.py:537
  202.2 1.8 copy-done.1
  204.0 4.7 %sum_all.1.refs_2_ = bf16[352,6144]{1,0:T(8,128)(2,1)} custom-call(bf16[2,352,2048]{2,1,0:T(8,128)(2,1)S(1)} %copy-done.1, bf16[2,352,2048]{2,1,0:T(8,128)(2,1)S(1)} %collective-permute-done.23.refs_1_, bf16[352,2048]{1,0:T(8,128)(2,1)S(1)} %copy-done.6, bf16[352,2048]{1,0:T(8,128)(2,1)} %collective-permute-done.22.refs_22_.refs_3_, ...), custom_call_target="tpu_custom_call" | custom-call | flops 1024 | bytes 67108864 | tf_op jit(solution)/shard_map/sum_all/pallas_call | solution.py:51
  208.7 2.2 %copy-done = bf16[352,6144]{1,0:T(8,128)(2,1)S(1)} copy-done((bf16[352,6144]{1,0:T(8,128)(2,1)S(1)}, bf16[352,6144]{1,0:T(8,128)(2,1)}, u32[]{:S(2)}) %copy-start) | copy-done | bytes 4325400
  (132 shorter events, 44.3 us)
Async XLA Ops:
  4.1 17.7 %collective-permute-start = (bf16[128,2176]{1,0:T(8,128)(2,1)S(1)}, bf16[128,2176]{1,0:T(8,128)(2,1)S(1)}, u32[]{:S(2)}, u32[]{:S(2)}) collective-permute-start(bf16[128,2176]{1,0:T(8,128)(2,1)S(1)} %get-tuple-element.47), channel_id=1, source_target_pairs={{0,8},{4,12},{8,24},{12,28},{24,16},{28,20},{16,0},{20,4},{1,9},{5... | collective-permute-start | bytes 1671176 | tf_op jit(solution)/shard_map/ppermute | solution.py:528
  8.7 13.1 %collective-permute-start.4 = (bf16[64,2048]{1,0:T(8,128)(2,1)S(1)}, bf16[64,2048]{1,0:T(8,128)(2,1)S(1)}, u32[]{:S(2)}, u32[]{:S(2)}) collective-permute-start(bf16[64,2048]{1,0:T(8,128)(2,1)S(1)} %get-tuple-element.50.refs_0_.refs_5_), channel_id=1, source_target_pairs={{0,2},{1,3},{2,0},{3,1},{4,6},{5,7},{6,4},{7,5},{8,10},{9,11},{10,... | collective-permute-start | bytes 786440 | tf_op jit(solution)/shard_map/ppermute | solution.py:537
  10.2 11.6 %collective-permute-start.5 = (bf16[64,2048]{1,0:T(8,128)(2,1)S(1)}, bf16[64,2048]{1,0:T(8,128)(2,1)S(1)}, u32[]{:S(2)}, u32[]{:S(2)}) collective-permute-start(bf16[64,2048]{1,0:T(8,128)(2,1)S(1)} %get-tuple-element.49), channel_id=1, source_target_pairs={{0,6},{1,7},{2,4},{3,5},{4,2},{5,3},{6,0},{7,1},{8,14},{9,15},{10,... | collective-permute-start | bytes 786440 | tf_op jit(solution)/shard_map/ppermute | solution.py:537
  24.2 15.8 %collective-permute-start.6 = (bf16[128,2048]{1,0:T(8,128)(2,1)S(1)}, bf16[128,2048]{1,0:T(8,128)(2,1)S(1)}, u32[]{:S(2)}, u32[]{:S(2)}) collective-permute-start(bf16[128,2048]{1,0:T(8,128)(2,1)S(1)} %get-tuple-element.53), channel_id=1, source_target_pairs={{0,8},{4,12},{8,24},{12,28},{24,16},{28,20},{16,0},{20,4},{1,9},{5... | collective-permute-start | bytes 1572872 | tf_op jit(solution)/shard_map/ppermute | solution.py:528
  26.9 25.1 %collective-permute-start.1 = (bf16[128,2176]{1,0:T(8,128)(2,1)S(1)}, bf16[128,2176]{1,0:T(8,128)(2,1)S(1)}, u32[]{:S(2)}, u32[]{:S(2)}) collective-permute-start(bf16[128,2176]{1,0:T(8,128)(2,1)S(1)} %collective-permute-done.refs_1_), channel_id=1, source_target_pairs={{0,8},{4,12},{8,24},{12,28},{24,16},{28,20},{16,0},{20,4},{1,9},{5... | collective-permute-start | bytes 1671176 | tf_op jit(solution)/shard_map/ppermute | solution.py:528
  27.3 14.9 %collective-permute-start.9 = (bf16[2,64,2048]{2,1,0:T(8,128)(2,1)S(1)}, bf16[2,64,2048]{2,1,0:T(8,128)(2,1)S(1)}, u32[]{:S(2)}, u32[]{:S(2)}) collective-permute-start(bf16[2,64,2048]{2,1,0:T(8,128)(2,1)S(1)} %get-tuple-element.56), channel_id=1, source_target_pairs={{0,4},{1,5},{2,6},{3,7},{4,0},{5,1},{6,2},{7,3},{8,12},{9,13},{10,... | collective-permute-start | bytes 1572872 | tf_op jit(solution)/shard_map/ppermute | solution.py:537
  28.8 22.0 %collective-permute-start.7 = (bf16[64,2048]{1,0:T(8,128)(2,1)S(1)}, bf16[64,2048]{1,0:T(8,128)(2,1)S(1)}, u32[]{:S(2)}, u32[]{:S(2)}) collective-permute-start(bf16[64,2048]{1,0:T(8,128)(2,1)S(1)} %get-tuple-element.54.refs_2_.refs_7_), channel_id=1, source_target_pairs={{0,2},{1,3},{2,0},{3,1},{4,6},{5,7},{6,4},{7,5},{8,10},{9,11},{10,... | collective-permute-start | bytes 786440 | tf_op jit(solution)/shard_map/ppermute | solution.py:537
  30.3 20.5 %collective-permute-start.8 = (bf16[64,2048]{1,0:T(8,128)(2,1)S(1)}, bf16[64,2048]{1,0:T(8,128)(2,1)S(1)}, u32[]{:S(2)}, u32[]{:S(2)}) collective-permute-start(bf16[64,2048]{1,0:T(8,128)(2,1)S(1)} %get-tuple-element.55), channel_id=1, source_target_pairs={{0,6},{1,7},{2,4},{3,5},{4,2},{5,3},{6,0},{7,1},{8,14},{9,15},{10,... | collective-permute-start | bytes 786440 | tf_op jit(solution)/shard_map/ppermute | solution.py:537
  40.0 23.2 %collective-permute-start.10 = (bf16[128,2048]{1,0:T(8,128)(2,1)S(1)}, bf16[128,2048]{1,0:T(8,128)(2,1)S(1)}, u32[]{:S(2)}, u32[]{:S(2)}) collective-permute-start(bf16[128,2048]{1,0:T(8,128)(2,1)S(1)} %collective-permute-done.6.refs_4_), channel_id=1, source_target_pairs={{0,8},{4,12},{8,24},{12,28},{24,16},{28,20},{16,0},{20,4},{1,9},{5... | collective-permute-start | bytes 1572872 | tf_op jit(solution)/shard_map/ppermute | solution.py:528
  53.1 14.9 %collective-permute-start.11 = (bf16[2,64,2048]{2,1,0:T(8,128)(2,1)S(1)}, bf16[2,64,2048]{2,1,0:T(8,128)(2,1)S(1)}, u32[]{:S(2)}, u32[]{:S(2)}) collective-permute-start(bf16[2,64,2048]{2,1,0:T(8,128)(2,1)S(1)} %get-tuple-element.62), channel_id=1, source_target_pairs={{0,4},{1,5},{2,6},{3,7},{4,0},{5,1},{6,2},{7,3},{8,12},{9,13},{10,... | collective-permute-start | bytes 1572872 | tf_op jit(solution)/shard_map/ppermute | solution.py:537
  54.3 26.2 %collective-permute-start.2 = (bf16[128,2176]{1,0:T(8,128)(2,1)S(1)}, bf16[128,2176]{1,0:T(8,128)(2,1)S(1)}, u32[]{:S(2)}, u32[]{:S(2)}) collective-permute-start(bf16[128,2176]{1,0:T(8,128)(2,1)S(1)} %collective-permute-done.1.refs_1_), channel_id=1, source_target_pairs={{0,8},{4,12},{8,24},{12,28},{24,16},{28,20},{16,0},{20,4},{1,9},{5... | collective-permute-start | bytes 1671176 | tf_op jit(solution)/shard_map/ppermute | solution.py:528
  57.0 11.1 %collective-permute-start.13 = (bf16[64,2048]{1,0:T(8,128)(2,1)S(1)}, bf16[64,2048]{1,0:T(8,128)(2,1)S(1)}, u32[]{:S(2)}, u32[]{:S(2)}) collective-permute-start(bf16[64,2048]{1,0:T(8,128)(2,1)S(1)} %get-tuple-element.65), channel_id=1, source_target_pairs={{0,6},{1,7},{2,4},{3,5},{4,2},{5,3},{6,0},{7,1},{8,14},{9,15},{10,... | collective-permute-start | bytes 786440 | tf_op jit(solution)/shard_map/ppermute | solution.py:537
  63.2 22.1 %collective-permute-start.15 = (bf16[128,2048]{1,0:T(8,128)(2,1)S(1)}, bf16[128,2048]{1,0:T(8,128)(2,1)S(1)}, u32[]{:S(2)}, u32[]{:S(2)}) collective-permute-start(bf16[128,2048]{1,0:T(8,128)(2,1)S(1)} %collective-permute-done.10.refs_4_), channel_id=1, source_target_pairs={{0,8},{4,12},{8,24},{12,28},{24,16},{28,20},{16,0},{20,4},{1,9},{5... | collective-permute-start | bytes 1572872 | tf_op jit(solution)/shard_map/ppermute | solution.py:528
  79.7 25.7 %collective-permute-start.17 = (bf16[1408,256]{1,0:T(8,128)(2,1)S(1)}, bf16[1408,256]{1,0:T(8,128)(2,1)S(1)}, u32[]{:S(2)}, u32[]{:S(2)}) collective-permute-start(bf16[1408,256]{1,0:T(8,128)(2,1)S(1)} %get-tuple-element.79), channel_id=1, source_target_pairs={{0,2},{1,3},{2,0},{3,1},{4,6},{5,7},{6,4},{7,5},{8,10},{9,11},{10,... | collective-permute-start | bytes 2162696 | tf_op jit(solution)/shard_map/ppermute | solution.py:537
  81.7 13.7 %collective-permute-start.14 = (bf16[2,64,2048]{2,1,0:T(8,128)(2,1)S(1)}, bf16[2,64,2048]{2,1,0:T(8,128)(2,1)S(1)}, u32[]{:S(2)}, u32[]{:S(2)}) collective-permute-start(bf16[2,64,2048]{2,1,0:T(8,128)(2,1)S(1)} %get-tuple-element.68), channel_id=1, source_target_pairs={{0,4},{1,5},{2,6},{3,7},{4,0},{5,1},{6,2},{7,3},{8,12},{9,13},{10,... | collective-permute-start | bytes 1572872 | tf_op jit(solution)/shard_map/ppermute | solution.py:537
  83.5 21.9 %collective-permute-start.18 = (bf16[64,2048]{1,0:T(8,128)(2,1)S(1)}, bf16[64,2048]{1,0:T(8,128)(2,1)S(1)}, u32[]{:S(2)}, u32[]{:S(2)}) collective-permute-start(bf16[64,2048]{1,0:T(8,128)(2,1)S(1)} %get-tuple-element.73.refs_2_.refs_11_), channel_id=1, source_target_pairs={{0,2},{1,3},{2,0},{3,1},{4,6},{5,7},{6,4},{7,5},{8,10},{9,11},{10,... | collective-permute-start | bytes 786440 | tf_op jit(solution)/shard_map/ppermute | solution.py:537
  84.8 20.6 %collective-permute-start.19 = (bf16[64,2048]{1,0:T(8,128)(2,1)S(1)}, bf16[64,2048]{1,0:T(8,128)(2,1)S(1)}, u32[]{:S(2)}, u32[]{:S(2)}) collective-permute-start(bf16[64,2048]{1,0:T(8,128)(2,1)S(1)} %get-tuple-element.80), channel_id=1, source_target_pairs={{0,6},{1,7},{2,4},{3,5},{4,2},{5,3},{6,0},{7,1},{8,14},{9,15},{10,... | collective-permute-start | bytes 786440 | tf_op jit(solution)/shard_map/ppermute | solution.py:537
  85.6 19.9 %collective-permute-start.16 = (bf16[64,2048]{1,0:T(8,128)(2,1)S(1)}, bf16[64,2048]{1,0:T(8,128)(2,1)S(1)}, u32[]{:S(2)}, u32[]{:S(2)}) collective-permute-start(bf16[64,2048]{1,0:T(8,128)(2,1)S(1)} %get-tuple-element.72.refs_5_), channel_id=1, source_target_pairs={{0,4},{1,5},{2,6},{3,7},{4,0},{5,1},{6,2},{7,3},{8,12},{9,13},{10,... | collective-permute-start | bytes 786440 | tf_op jit(solution)/shard_map/ppermute | solution.py:537
  112.1 24.8 %collective-permute-start.21 = (bf16[352,2048]{1,0:T(8,128)(2,1)}, bf16[352,2048]{1,0:T(8,128)(2,1)}, u32[]{:S(2)}, u32[]{:S(2)}) collective-permute-start(bf16[352,2048]{1,0:T(8,128)(2,1)} %get-tuple-element.86), channel_id=1, source_target_pairs={{0,1},{1,0},{2,3},{3,2},{4,5},{5,4},{6,7},{7,6},{8,9},{9,8},{10,11... | collective-permute-start | bytes 4325384 | tf_op jit(solution)/shard_map/ppermute | solution.py:537
  112.1 41.3 %collective-permute-start.22 = (bf16[352,2048]{1,0:T(8,128)(2,1)}, bf16[352,2048]{1,0:T(8,128)(2,1)}, u32[]{:S(2)}, u32[]{:S(2)}) collective-permute-start(bf16[352,2048]{1,0:T(8,128)(2,1)} %get-tuple-element.87), channel_id=1, source_target_pairs={{0,1},{1,0},{2,3},{3,2},{4,5},{5,4},{6,7},{7,6},{8,9},{9,8},{10,11... | collective-permute-start | bytes 4325384 | tf_op jit(solution)/shard_map/ppermute | solution.py:537
  128.8 79.9 %all-to-all-start = ((bf16[8,64,2048]{2,1,0:T(8,128)(2,1)}), bf16[8,64,2048]{2,1,0:T(8,128)(2,1)S(1)}, u32[]{:S(2)}, u32[]{:S(2)}) async-start(bf16[8,64,2048]{2,1,0:T(8,128)(2,1)} %copy-done.4), calls=%async_computation | async-start | bytes 4194304 | tf_op jit(solution)/shard_map/all_to_all | solution.py:597
  135.4 18.0 %collective-permute-start.20 = (bf16[1408,256]{1,0:T(8,128)(2,1)}, bf16[1408,256]{1,0:T(8,128)(2,1)S(1)}, u32[]{:S(2)}, u32[]{:S(2)}) collective-permute-start(bf16[1408,256]{1,0:T(8,128)(2,1)} %copy-done.42), channel_id=1, source_target_pairs={{0,2},{1,3},{2,0},{3,1},{4,6},{5,7},{6,4},{7,5},{8,10},{9,11},{10,... | collective-permute-start | bytes 2162696 | tf_op jit(solution)/shard_map/ppermute | solution.py:537
  168.2 34.0 %collective-permute-start.23 = (bf16[2,352,2048]{2,1,0:T(8,128)(2,1)}, bf16[2,352,2048]{2,1,0:T(8,128)(2,1)S(1)}, u32[]{:S(2)}, u32[]{:S(2)}) collective-permute-start(bf16[2,352,2048]{2,1,0:T(8,128)(2,1)} %get-tuple-element.89), channel_id=1, source_target_pairs={{0,1},{1,0},{2,3},{3,2},{4,5},{5,4},{6,7},{7,6},{8,9},{9,8},{10,11... | collective-permute-start | bytes 8650760 | tf_op jit(solution)/shard_map/ppermute | solution.py:537
  168.2 34.0 %collective-permute-start.24 = (bf16[352,2048]{1,0:T(8,128)(2,1)S(1)}, bf16[352,2048]{1,0:T(8,128)(2,1)S(1)}, u32[]{:S(2)}, u32[]{:S(2)}) collective-permute-start(bf16[352,2048]{1,0:T(8,128)(2,1)S(1)} %add_convert_fusion.refs_21_), channel_id=1, source_target_pairs={{0,2},{1,3},{2,0},{3,1},{4,6},{5,7},{6,4},{7,5},{8,10},{9,11},{10,... | collective-permute-start | bytes 4325384 | tf_op jit(solution)/shard_map/ppermute | solution.py:537
  (45 other events, 505.8 us)
where the time goes:
time: 213 us; the launch traced here: 212 us
  waiting for transfers between devices  84 us (39%)
  Pallas kernels  66.2 us (31%)
  starting transfers between devices  38.1 us (18%)
  local copies, waits for them, and re-layouts  18.8 us (9%)
  other arithmetic  3.91 us (2%)
    ppermute x19, waiting for transfers between devices, across(): return lax.ppermute(value, ('expert', 'replica'), pairs)  68.9 us
    pallas_call x14, Pallas kernels, call(): pl.pallas_call(body_of, in_specs=list(specs) + [anywhere()] * len(extra),...  66.2 us
    ppermute x19, starting transfers between devices, across(): return lax.ppermute(value, ('expert', 'replica'), pairs)  20.3 us
    unnamed x86, local copies, waits for them, and re-layouts  18.7 us
    ppermute x6, waiting for transfers between devices, along_ring(): return lax.ppermute(value, 'expert', pairs)  15.1 us
    ppermute x6, starting transfers between devices, along_ring(): return lax.ppermute(value, 'expert', pairs)  11.3 us
    all_to_all x1, starting transfers between devices, body(): lax.all_to_all(dx, 'expert', split_axis=0, concat_axis=0, tiled=True)  6.55 us
  transfers between devices with their start and end apart: 26, of which 10 were waited for; matrix products, arithmetic and copies ran while one was open for 1% of the time, Pallas kernels for 27%

commit v1 on v0

--- a/solution.py
+++ b/solution.py
@@ -35,6 +35,10 @@
 
 def tile_of(width, most):
     return most if width % most == 0 else width
+
+
+def large_cost():
+    return pl.CostEstimate(flops=40 * 10**9, bytes_accessed=1 << 27, transcendentals=0)
 
 
 class Order:
@@ -291,7 +295,7 @@
         slope_ref[t] = up * sig * (1.0 + gate * (1.0 - sig))
 
 
-def gate_up(order, pieces, w_stack, capacity, deps=()):
+def gate_up(order, pieces, w_stack, capacity, cost=None):
     arrays, whiches = split_pieces(pieces)
     width = arrays[0].shape[-1]
     rows, hidden = len(pieces) * capacity, w_stack.shape[1]
@@ -299,7 +303,7 @@
         functools.partial(gate_up_kernel, whiches),
         [anywhere()] * (len(pieces) + 1),
         [*arrays, w_stack],
-        deps,
+        cost=cost,
         out_specs=[inside()] * 3,
         out_shape=[
             jax.ShapeDtypeStruct((2, hidden // 2, rows), BF16),
@@ -380,6 +384,7 @@
         specs,
         operands,
         deps,
+        None if dx is None else large_cost(),
         out_specs=[anywhere(), inside(), inside()],
         out_shape=[jax.ShapeDtypeStruct(shape, BF16)]
         + [jax.ShapeDtypeStruct((hidden, rows), BF16)] * 2,
@@ -408,8 +413,9 @@
 
 
 def grad_x_kernel(act_count, whiches, place_ref, *refs):
-    acts, rows = refs[:act_count], refs[act_count:-2]
-    send_ref, keep_ref = refs[-2:]
+    acts, rows = refs[:act_count], refs[act_count:-4]
+    send_ref, keep_ref, right, sems = refs[-4:]
+    copies = start_rows(list(zip(rows, whiches)), right, sems)
     own, width = send_ref.shape[1:]
     low = place_ref[3]
     lefts = []
@@ -418,11 +424,12 @@
             start = pl.multiple_of((2 * lead + who) * own, own)
             lefts.append(jnp.concatenate([ref[pl.ds(start, own), :] for ref in acts], axis=1))
     left = jnp.concatenate(lefts, axis=0)
+    for copy in copies:
+        copy.wait()
     tile = tile_of(width, 512)
     for n in range(0, width, tile):
         columns = slice(n, n + tile)
-        right = side_by_side(rows, whiches, columns)
-        total = jnp.dot(left, right, preferred_element_type=F32).astype(BF16)
+        total = jnp.dot(left, right[:, columns], preferred_element_type=F32).astype(BF16)
         for lead in range(2):
             send_ref[lead, :, columns] = total[lead * own : (lead + 1) * own]
             keep_ref[lead, :, columns] = total[(2 + lead) * own : (3 + lead) * own]
@@ -433,9 +440,14 @@
     arrays, whiches = split_pieces(rows)
     return order.call(
         functools.partial(grad_x_kernel, len(acts), whiches),
-        [smem()] + [inside()] * (len(acts) + len(rows)),
+        [smem()] + [inside()] * len(acts) + [anywhere()] * len(rows),
         [place, *acts, *arrays],
         deps,
+        large_cost(),
+        scratch_shapes=[
+            pltpu.VMEM((sum(act.shape[1] for act in acts), width), BF16),
+            pltpu.SemaphoreType.DMA((len(rows),)),
+        ],
         out_specs=[inside()] * 2,
         out_shape=[jax.ShapeDtypeStruct((2, own, width), BF16)] * 2,
         name="grad_x",
@@ -477,25 +489,39 @@
     )
 
 
-def sum_kernel(down_count, keep_ref, come_ref, *refs):
-    downs, out_ref = refs[:down_count], refs[down_count]
+def sum_down_kernel(*refs):
+    total = refs[0][...].astype(F32)
+    for ref in refs[1:-1]:
+        total = total + ref[...].astype(F32)
+    refs[-1][...] = total.astype(BF16)
+
+
+def sum_down(order, terms):
+    return order.call(
+        sum_down_kernel,
+        [inside()] * len(terms),
+        terms,
+        cost=large_cost(),
+        out_specs=inside(),
+        out_shape=jax.ShapeDtypeStruct(terms[0].shape, BF16),
+        name="sum_down",
+    )
+
+
+def sum_kernel(keep_ref, come_ref, down_ref, out_ref):
     width = keep_ref.shape[2]
     for lead in range(2):
         total = keep_ref[lead].astype(F32) + come_ref[lead].astype(F32)
         out_ref[:, lead * width : (lead + 1) * width] = total.astype(BF16)
-    total = downs[0][...].astype(F32)
-    for ref in downs[1:]:
-        total = total + ref[...].astype(F32)
-    out_ref[:, 2 * width :] = total.astype(BF16)
-
-
-def sum_all(order, keep, come, downs):
+    out_ref[:, 2 * width :] = down_ref[...]
+
+
+def sum_all(order, keep, come, down):
     _, own, width = keep.shape
     return order.call(
-        functools.partial(sum_kernel, len(downs)),
-        [inside()] * (2 + len(downs)),
-        [keep, come, *downs],
-        cost=pl.CostEstimate(flops=1024, bytes_accessed=1 << 26, transcendentals=0),
+        sum_kernel,
+        [inside()] * 3,
+        [keep, come, down],
         out_specs=inside(),
         out_shape=jax.ShapeDtypeStruct((own, 3 * width), BF16),
         name="sum_all",
@@ -558,7 +584,7 @@
         waits = {
             1: [value for value, _ in x_pieces[1:] + x_other],
             2: [value for value, _ in x_other[columns:]],
-            3: [],
+            3: [value for value, _ in x_other[2 * columns :]],
         }[s]
         d_next = along_ring(d_block) if s > 1 else None
         keep_x, keep_d, pairs, sends, again, scales, hits = select_both(
@@ -574,23 +600,23 @@
         if s == 1:
             hid, *factors = gate_up(order, x_pieces[: 2 * columns], w_stack, capacity)
             hids.append(hid)
-        if s == 2:
+        if s == 3:
             dx, send, keep = backward(
                 order, place, dy_pieces[: 2 * columns], *factors, w_stack, columns, 0, None,
-                dx_shape, [value for value, _ in x_other[2 * columns : 3 * columns]],
+                dx_shape, [],
             )
             acts_kept.append(keep)
             acts_come.append(across(send, 0, 2))
     picked = select_last(order, scales, hits, d_block, columns, [])
     dy_pieces += [(picked[0], None)] + [(value, None) for value in exchange(picked[1:], 0)]
-    hid, *factors = gate_up(order, x_pieces[2 * columns :], w_stack, capacity)
+    hid, *factors = gate_up(order, x_pieces[2 * columns :], w_stack, capacity, large_cost())
     hids.append(hid)
     send_other, keep_other, send_own, down_own = grad_down(
-        order, place, hids, dy_pieces, width,
-        [acts_come[0]] + [value for value, _ in x_other[3 * columns :]],
+        order, place, hids, dy_pieces, width, []
     )
     dx, send, keep = backward(
-        order, place, dy_pieces[2 * columns :], *factors, w_stack, columns, 2, dx, dx_shape, [],
+        order, place, dy_pieces[2 * columns :], *factors, w_stack, columns, 2, dx, dx_shape,
+        [value for value, _ in x_other[3 * columns :]],
     )
     acts_kept.append(keep)
     acts_come.append(across(send, 0, 2))
@@ -603,7 +629,8 @@
     send, keep = grad_x(
         order, place, acts_kept + acts_come, x_pieces + x_other, width, [summed, down_core]
     )
-    g_rows = sum_all(order, keep, across(send, 0, 1), [down_own, down_core, down_y])
+    down = sum_down(order, [down_own, down_core, down_y])
+    g_rows = sum_all(order, keep, across(send, 0, 1), down)
     d_tokens = merge(order, all_hits, returned.reshape(experts * capacity, width))
     return d_tokens, g_rows[None]
 

time: 213 us -> 187 us (0.88)
  waiting for transfers between devices: 84 us -> 63.9 us
  local copies, waits for them, and re-layouts: 18.8 us -> 13.1 us
  starting transfers between devices: 38.1 us -> 34.9 us
  Pallas kernels: 66.2 us -> 69.1 us
    ppermute x19, waiting for transfers between devices: 68.9 us -> 31.1 us  [across(): return lax.ppermute(value, ('expert', 'replica'), pairs)]
    ppermute x6, waiting for transfers between devices: 15.1 us -> 32.8 us  [along_ring(): return lax.ppermute(value, 'expert', pairs)]
    unnamed x86, local copies, waits for them, and re-layouts: 18.7 us -> 13 us
    pallas_call x14 -> x15, Pallas kernels: 66.2 us -> 69.1 us  [call(): pl.pallas_call(body_of, in_specs=list(specs) + [anywhere()] * len(extra),...]
  transfers between devices with their start and end apart: 26 -> 26, of which waited for: 10 -> 8; matrix products, arithmetic and copies ran while one was open for 1% -> 1% of each run, Pallas kernels for 27% -> 36%
where the time goes in v1:
time: 187 us; the launch traced here: 186 us
  Pallas kernels  69.1 us (37%)
  waiting for transfers between devices  63.9 us (34%)
  starting transfers between devices  34.9 us (19%)
  local copies, waits for them, and re-layouts  13.1 us (7%)
  other arithmetic  3.95 us (2%)
    pallas_call x15, Pallas kernels, call(): pl.pallas_call(body_of, in_specs=list(specs) + [anywhere()] * len(extra),...  69.1 us
    ppermute x6, waiting for transfers between devices, along_ring(): return lax.ppermute(value, 'expert', pairs)  32.8 us
    ppermute x19, waiting for transfers between devices, across(): return lax.ppermute(value, ('expert', 'replica'), pairs)  31.1 us
    ppermute x19, starting transfers between devices, across(): return lax.ppermute(value, ('expert', 'replica'), pairs)  20.7 us
    unnamed x86, local copies, waits for them, and re-layouts  13 us
    ppermute x6, starting transfers between devices, along_ring(): return lax.ppermute(value, 'expert', pairs)  9.52 us
    all_to_all x1, starting transfers between devices, body(): lax.all_to_all(dx, 'expert', split_axis=0, concat_axis=0, tiled=True)  4.66 us
  transfers between devices with their start and end apart: 26, of which 8 were waited for; matrix products, arithmetic and copies ran while one was open for 1% of the time, Pallas kernels for 36%

profile of v1, /device:TPU:0, one launch (start us, length us, event | category | flops | bytes accessed | tf_op | source)
XLA Modules:
  0.0 186.3 jit_solution(5572410898156395633)
XLA Ops:
  4.1 3.1 %collective-permute-start = (bf16[128,2176]{1,0:T(8,128)(2,1)S(1)}, bf16[128,2176]{1,0:T(8,128)(2,1)S(1)}, u32[]{:S(2)}, u32[]{:S(2)}) collective-permute-start(bf16[128,2176]{1,0:T(8,128)(2,1)S(1)} %get-tuple-element.47), channel_id=1, source_target_pairs={{0,8},{4,12},{8,24},{12,28},{24,16},{28,20},{16,0},{20,4},{1,9},{5... | collective-permute-start | bytes 1671176 | tf_op jit(solution)/shard_map/ppermute | solution.py:554
  10.7 10.2 %collective-permute-done.refs_1_ = bf16[128,2176]{1,0:T(8,128)(2,1)S(1)} collective-permute-done((bf16[128,2176]{1,0:T(8,128)(2,1)S(1)}, bf16[128,2176]{1,0:T(8,128)(2,1)S(1)}, u32[]{:S(2)}, u32[]{:S(2)}) %collective-permute-start) | collective-permute-done | bytes 557088 | tf_op jit(solution)/shard_map/ppermute | solution.py:554
  24.3 3.4 %collective-permute-start.6 = (bf16[128,2048]{1,0:T(8,128)(2,1)S(1)}, bf16[128,2048]{1,0:T(8,128)(2,1)S(1)}, u32[]{:S(2)}, u32[]{:S(2)}) collective-permute-start(bf16[128,2048]{1,0:T(8,128)(2,1)S(1)} %get-tuple-element.53), channel_id=1, source_target_pairs={{0,8},{4,12},{8,24},{12,28},{24,16},{28,20},{16,0},{20,4},{1,9},{5... | collective-permute-start | bytes 1572872 | tf_op jit(solution)/shard_map/ppermute | solution.py:554
  29.2 8.1 %collective-permute-done.1.refs_1_ = bf16[128,2176]{1,0:T(8,128)(2,1)S(1)} collective-permute-done((bf16[128,2176]{1,0:T(8,128)(2,1)S(1)}, bf16[128,2176]{1,0:T(8,128)(2,1)S(1)}, u32[]{:S(2)}, u32[]{:S(2)}) %collective-permute-start.1) | collective-permute-done | bytes 557088 | tf_op jit(solution)/shard_map/ppermute | solution.py:554
  41.1 7.4 %collective-permute-done.6.refs_4_ = bf16[128,2048]{1,0:T(8,128)(2,1)S(1)} collective-permute-done((bf16[128,2048]{1,0:T(8,128)(2,1)S(1)}, bf16[128,2048]{1,0:T(8,128)(2,1)S(1)}, u32[]{:S(2)}, u32[]{:S(2)}) %collective-permute-start.6) | collective-permute-done | bytes 524320 | tf_op jit(solution)/shard_map/ppermute | solution.py:554
  49.4 8.6 %gate_up.2 = (bf16[2,704,256]{2,1,0:T(8,128)(2,1)S(1)}, f32[2,704,256]{2,1,0:T(8,128)S(1)}, f32[2,704,256]{2,1,0:T(8,128)S(1)}) custom-call(bf16[64,2048]{1,0:T(8,128)(2,1)S(1)} %get-tuple-element.50.refs_0_.refs_5_, bf16[64,2048]{1,0:T(8,128)(2,1)S(1)} %collective-permute-done.3.refs_5_.refs_1_.refs_6_, ...), custom_call_target="tpu_custom_call" | custom-call | flops 1024 | bytes 1024 | tf_op jit(solution)/shard_map/gate_up/pallas_call | solution.py:55
  59.3 1.6 collective-permute-start.11
  62.9 7.1 %collective-permute-done.10.refs_4_ = bf16[128,2048]{1,0:T(8,128)(2,1)S(1)} collective-permute-done((bf16[128,2048]{1,0:T(8,128)(2,1)S(1)}, bf16[128,2048]{1,0:T(8,128)(2,1)S(1)}, u32[]{:S(2)}, u32[]{:S(2)}) %collective-permute-start.10) | collective-permute-done | bytes 524320 | tf_op jit(solution)/shard_map/ppermute | solution.py:554
  72.2 1.6 collective-permute-start.13
  75.7 3.6 %collective-permute-done.15.refs_4_.refs_1_.refs_6_.refs_10_ = bf16[2,64,2048]{2,1,0:T(8,128)(2,1)S(1)} collective-permute-done((bf16[2,64,2048]{2,1,0:T(8,128)(2,1)S(1)}, bf16[2,64,2048]{2,1,0:T(8,128)(2,1)S(1)}, u32[]{:S(2)}, u32[]{:S(2)}) %collective-permute-start.15) | collective-permute-done | bytes 524320 | tf_op jit(solution)/shard_map/ppermute | solution.py:563
  79.4 12.5 %backward.2 = (bf16[8,64,2048]{2,1,0:T(8,128)(2,1)S(1)}, bf16[1408,256]{1,0:T(8,128)(2,1)}, bf16[1408,256]{1,0:T(8,128)(2,1)S(1)}) custom-call(s32[8]{0:T(128)S(1)} %stack.35.refs_0_, bf16[64,2048]{1,0:T(8,128)(2,1)S(1)} %get-tuple-element.66.refs_1_.refs_3_, bf16[2,64,2048]{2,1,0:T(8,128)(2,1)S(1)} %collective-permute-done.9.refs_3_.refs_2_.refs_4_.refs_8_, ...), custom_call_target="tpu_custom_call" | custom-call | flops 1024 | bytes 1024 | tf_op jit(solution)/shard_map/backward/pallas_call | solution.py:55
  95.3 8.9 %gate_up.3 = (bf16[2,704,256]{2,1,0:T(8,128)(2,1)S(1)}, f32[2,704,256]{2,1,0:T(8,128)S(1)}, f32[2,704,256]{2,1,0:T(8,128)S(1)}) custom-call(bf16[64,2048]{1,0:T(8,128)(2,1)S(1)} %get-tuple-element.60.refs_0_.refs_9_, bf16[2,64,2048]{2,1,0:T(8,128)(2,1)S(1)} %collective-permute-done.15.refs_4_.refs_1_.refs_6_.refs_10_, ...), custom_call_target="tpu_custom_call" | custom-call | flops 40000000000 | bytes 134217728 | tf_op jit(solution)/shard_map/gate_up/pallas_call | solution.py:55
  105.2 5.0 %grad_down.1 = (bf16[352,2048]{1,0:T(8,128)(2,1)}, bf16[352,2048]{1,0:T(8,128)(2,1)S(1)}, bf16[352,2048]{1,0:T(8,128)(2,1)}, bf16[352,2048]{1,0:T(8,128)(2,1)S(1)}) custom-call(s32[8]{0:T(128)S(1)} %stack.35.refs_0_, bf16[2,704,256]{2,1,0:T(8,128)(2,1)S(1)} %get-tuple-element.78.refs_1_, bf16[2,704,256]{2,1,0:T(8,128)(2,1)S(1)} %get-tuple-element.79.refs_2_, ...), custom_call_target="tpu_custom_call" | custom-call | flops 1024 | bytes 1024 | tf_op jit(solution)/shard_map/grad_down/pallas_call | solution.py:55
  111.9 12.7 %backward.3 = (bf16[8,64,2048]{2,1,0:T(8,128)(2,1)S(1)}, bf16[1408,256]{1,0:T(8,128)(2,1)}, bf16[1408,256]{1,0:T(8,128)(2,1)S(1)}) custom-call(s32[8]{0:T(128)S(1)} %stack.35.refs_0_, bf16[64,2048]{1,0:T(8,128)(2,1)S(1)} %get-tuple-element.62.refs_7_.refs_1_, ...), custom_call_target="tpu_custom_call", output_to_operand_aliasing={{0}: (8, {})} | custom-call | flops 40000000000 | bytes 134217728 | tf_op jit(solution)/shard_map/backward/pallas_call | solution.py:55
  127.3 4.7 %all-to-all-start = ((bf16[8,64,2048]{2,1,0:T(8,128)(2,1)}), bf16[8,64,2048]{2,1,0:T(8,128)(2,1)S(1)}, u32[]{:S(2)}, u32[]{:S(2)}) async-start(bf16[8,64,2048]{2,1,0:T(8,128)(2,1)} %copy-done.3), calls=%async_computation | async-start | bytes 4194304 | tf_op jit(solution)/shard_map/all_to_all | solution.py:623
  132.1 2.6 %add_convert_fusion.refs_21_ = bf16[352,2048]{1,0:T(8,128)(2,1)S(1)} fusion(bf16[352,2048]{1,0:T(8,128)(2,1)} %collective-permute-done.21, bf16[352,2048]{1,0:T(8,128)(2,1)} %copy-done.4), kind=kLoop, calls=%fused_computation | loop fusion | flops 2883584 | bytes 4325376 | tf_op jit(solution)/shard_map/convert_element_type | solution.py:625
  134.7 1.6 collective-permute-start.24
  136.3 9.8 %collective-permute-done.20.refs_4_ = bf16[1408,256]{1,0:T(8,128)(2,1)} collective-permute-done((bf16[1408,256]{1,0:T(8,128)(2,1)}, bf16[1408,256]{1,0:T(8,128)(2,1)}, u32[]{:S(2)}, u32[]{:S(2)}) %collective-permute-start.20) | collective-permute-done | bytes 720928 | tf_op jit(solution)/shard_map/ppermute | solution.py:563
  148.3 10.6 %grad_x.1 = (bf16[2,352,2048]{2,1,0:T(8,128)(2,1)}, bf16[2,352,2048]{2,1,0:T(8,128)(2,1)}) custom-call(s32[8]{0:T(128)S(1)} %stack.35.refs_0_, bf16[1408,256]{1,0:T(8,128)(2,1)S(1)} %copy-done.10, bf16[1408,256]{1,0:T(8,128)(2,1)S(1)} %copy-done.42, bf16[1408,256]{1,0:T(8,128)(2,1)} %collective-permute-done.19.refs_3_, ...), custom_call_target="tpu_custom_call" | custom-call | flops 40000000000 | bytes 134217728 | tf_op jit(solution)/shard_map/grad_x/pallas_call | solution.py:55
  159.0 17.0 %collective-permute-done.24.refs_2_ = bf16[352,2048]{1,0:T(8,128)(2,1)S(1)} collective-permute-done((bf16[352,2048]{1,0:T(8,128)(2,1)S(1)}, bf16[352,2048]{1,0:T(8,128)(2,1)S(1)}, u32[]{:S(2)}, u32[]{:S(2)}) %collective-permute-start.24) | collective-permute-done | bytes 1441824 | tf_op jit(solution)/shard_map/ppermute | solution.py:563
  176.0 1.8 copy-done.1
  177.8 2.0 %sum_down.1.refs_2_.refs_3_ = bf16[352,2048]{1,0:T(8,128)(2,1)S(1)} custom-call(bf16[352,2048]{1,0:T(8,128)(2,1)S(1)} %copy-done.32, bf16[352,2048]{1,0:T(8,128)(2,1)} %collective-permute-done.22.refs_22_.refs_1_, bf16[352,2048]{1,0:T(8,128)(2,1)S(1)} %collective-permute-done.24.refs_2_, bf16[2,352,2048]{2,1,0:T(8,128)(2,1)S(1)} %copy-done.1), custom_call_target="tpu_custom_call" | custom-call | flops 40000000000 | bytes 134217728 | tf_op jit(solution)/shard_map/sum_down/pallas_call | solution.py:55
  180.1 2.8 %sum_all.1.refs_2_ = bf16[352,6144]{1,0:T(8,128)(2,1)} custom-call(bf16[2,352,2048]{2,1,0:T(8,128)(2,1)S(1)} %copy-done.2, bf16[2,352,2048]{2,1,0:T(8,128)(2,1)S(1)} %collective-permute-done.23.refs_1_, bf16[352,2048]{1,0:T(8,128)(2,1)S(1)} %sum_down.1.refs_2_.refs_3_, bf16[352,2048]{1,0:T(8,128)(2,1)S(1)} %sum_down.1.refs_2_.refs_3_), custom_call_target="tpu_custom_call" | custom-call | flops 1024 | bytes 1024 | tf_op jit(solution)/shard_map/sum_all/pallas_call | solution.py:55
  182.8 2.2 %copy-done = bf16[352,6144]{1,0:T(8,128)(2,1)S(1)} copy-done((bf16[352,6144]{1,0:T(8,128)(2,1)S(1)}, bf16[352,6144]{1,0:T(8,128)(2,1)}, u32[]{:S(2)}) %copy-start) | copy-done | bytes 4325400
  (133 shorter events, 36.1 us)
Async XLA Ops:
  4.1 16.7 %collective-permute-start = (bf16[128,2176]{1,0:T(8,128)(2,1)S(1)}, bf16[128,2176]{1,0:T(8,128)(2,1)S(1)}, u32[]{:S(2)}, u32[]{:S(2)}) collective-permute-start(bf16[128,2176]{1,0:T(8,128)(2,1)S(1)} %get-tuple-element.47), channel_id=1, source_target_pairs={{0,8},{4,12},{8,24},{12,28},{24,16},{28,20},{16,0},{20,4},{1,9},{5... | collective-permute-start | bytes 1671176 | tf_op jit(solution)/shard_map/ppermute | solution.py:554
  7.2 14.7 %collective-permute-start.3 = (bf16[64,2048]{1,0:T(8,128)(2,1)S(1)}, bf16[64,2048]{1,0:T(8,128)(2,1)S(1)}, u32[]{:S(2)}, u32[]{:S(2)}) collective-permute-start(bf16[64,2048]{1,0:T(8,128)(2,1)S(1)} %get-tuple-element.49), channel_id=1, source_target_pairs={{0,4},{1,5},{2,6},{3,7},{4,0},{5,1},{6,2},{7,3},{8,12},{9,13},{10,... | collective-permute-start | bytes 786440 | tf_op jit(solution)/shard_map/ppermute | solution.py:563
  8.7 13.2 %collective-permute-start.4 = (bf16[64,2048]{1,0:T(8,128)(2,1)S(1)}, bf16[64,2048]{1,0:T(8,128)(2,1)S(1)}, u32[]{:S(2)}, u32[]{:S(2)}) collective-permute-start(bf16[64,2048]{1,0:T(8,128)(2,1)S(1)} %get-tuple-element.50.refs_0_.refs_5_), channel_id=1, source_target_pairs={{0,2},{1,3},{2,0},{3,1},{4,6},{5,7},{6,4},{7,5},{8,10},{9,11},{10,... | collective-permute-start | bytes 786440 | tf_op jit(solution)/shard_map/ppermute | solution.py:563
  10.2 11.7 %collective-permute-start.5 = (bf16[64,2048]{1,0:T(8,128)(2,1)S(1)}, bf16[64,2048]{1,0:T(8,128)(2,1)S(1)}, u32[]{:S(2)}, u32[]{:S(2)}) collective-permute-start(bf16[64,2048]{1,0:T(8,128)(2,1)S(1)} %get-tuple-element.49), channel_id=1, source_target_pairs={{0,6},{1,7},{2,4},{3,5},{4,2},{5,3},{6,0},{7,1},{8,14},{9,15},{10,... | collective-permute-start | bytes 786440 | tf_op jit(solution)/shard_map/ppermute | solution.py:563
  20.9 16.5 %collective-permute-start.1 = (bf16[128,2176]{1,0:T(8,128)(2,1)S(1)}, bf16[128,2176]{1,0:T(8,128)(2,1)S(1)}, u32[]{:S(2)}, u32[]{:S(2)}) collective-permute-start(bf16[128,2176]{1,0:T(8,128)(2,1)S(1)} %collective-permute-done.refs_1_), channel_id=1, source_target_pairs={{0,8},{4,12},{8,24},{12,28},{24,16},{28,20},{16,0},{20,4},{1,9},{5... | collective-permute-start | bytes 1671176 | tf_op jit(solution)/shard_map/ppermute | solution.py:554
  24.3 24.2 %collective-permute-start.6 = (bf16[128,2048]{1,0:T(8,128)(2,1)S(1)}, bf16[128,2048]{1,0:T(8,128)(2,1)S(1)}, u32[]{:S(2)}, u32[]{:S(2)}) collective-permute-start(bf16[128,2048]{1,0:T(8,128)(2,1)S(1)} %get-tuple-element.53), channel_id=1, source_target_pairs={{0,8},{4,12},{8,24},{12,28},{24,16},{28,20},{16,0},{20,4},{1,9},{5... | collective-permute-start | bytes 1572872 | tf_op jit(solution)/shard_map/ppermute | solution.py:554
  27.7 21.6 %collective-permute-start.9 = (bf16[2,64,2048]{2,1,0:T(8,128)(2,1)S(1)}, bf16[2,64,2048]{2,1,0:T(8,128)(2,1)S(1)}, u32[]{:S(2)}, u32[]{:S(2)}) collective-permute-start(bf16[2,64,2048]{2,1,0:T(8,128)(2,1)S(1)} %get-tuple-element.56), channel_id=1, source_target_pairs={{0,4},{1,5},{2,6},{3,7},{4,0},{5,1},{6,2},{7,3},{8,12},{9,13},{10,... | collective-permute-start | bytes 1572872 | tf_op jit(solution)/shard_map/ppermute | solution.py:563
  37.3 33.7 %collective-permute-start.2 = (bf16[128,2176]{1,0:T(8,128)(2,1)S(1)}, bf16[128,2176]{1,0:T(8,128)(2,1)S(1)}, u32[]{:S(2)}, u32[]{:S(2)}) collective-permute-start(bf16[128,2176]{1,0:T(8,128)(2,1)S(1)} %collective-permute-done.1.refs_1_), channel_id=1, source_target_pairs={{0,8},{4,12},{8,24},{12,28},{24,16},{28,20},{16,0},{20,4},{1,9},{5... | collective-permute-start | bytes 1671176 | tf_op jit(solution)/shard_map/ppermute | solution.py:554
  38.2 19.9 %collective-permute-start.7 = (bf16[64,2048]{1,0:T(8,128)(2,1)S(1)}, bf16[64,2048]{1,0:T(8,128)(2,1)S(1)}, u32[]{:S(2)}, u32[]{:S(2)}) collective-permute-start(bf16[64,2048]{1,0:T(8,128)(2,1)S(1)} %get-tuple-element.54.refs_2_.refs_7_), channel_id=1, source_target_pairs={{0,2},{1,3},{2,0},{3,1},{4,6},{5,7},{6,4},{7,5},{8,10},{9,11},{10,... | collective-permute-start | bytes 786440 | tf_op jit(solution)/shard_map/ppermute | solution.py:563
  39.7 18.4 %collective-permute-start.8 = (bf16[64,2048]{1,0:T(8,128)(2,1)S(1)}, bf16[64,2048]{1,0:T(8,128)(2,1)S(1)}, u32[]{:S(2)}, u32[]{:S(2)}) collective-permute-start(bf16[64,2048]{1,0:T(8,128)(2,1)S(1)} %get-tuple-element.55), channel_id=1, source_target_pairs={{0,6},{1,7},{2,4},{3,5},{4,2},{5,3},{6,0},{7,1},{8,14},{9,15},{10,... | collective-permute-start | bytes 786440 | tf_op jit(solution)/shard_map/ppermute | solution.py:563
  48.6 21.4 %collective-permute-start.10 = (bf16[128,2048]{1,0:T(8,128)(2,1)S(1)}, bf16[128,2048]{1,0:T(8,128)(2,1)S(1)}, u32[]{:S(2)}, u32[]{:S(2)}) collective-permute-start(bf16[128,2048]{1,0:T(8,128)(2,1)S(1)} %collective-permute-done.6.refs_4_), channel_id=1, source_target_pairs={{0,8},{4,12},{8,24},{12,28},{24,16},{28,20},{16,0},{20,4},{1,9},{5... | collective-permute-start | bytes 1572872 | tf_op jit(solution)/shard_map/ppermute | solution.py:554
  62.3 17.1 %collective-permute-start.15 = (bf16[2,64,2048]{2,1,0:T(8,128)(2,1)S(1)}, bf16[2,64,2048]{2,1,0:T(8,128)(2,1)S(1)}, u32[]{:S(2)}, u32[]{:S(2)}) collective-permute-start(bf16[2,64,2048]{2,1,0:T(8,128)(2,1)S(1)} %get-tuple-element.68), channel_id=1, source_target_pairs={{0,4},{1,5},{2,6},{3,7},{4,0},{5,1},{6,2},{7,3},{8,12},{9,13},{10,... | collective-permute-start | bytes 1572872 | tf_op jit(solution)/shard_map/ppermute | solution.py:563
  70.0 23.4 %collective-permute-start.14 = (bf16[128,2048]{1,0:T(8,128)(2,1)S(1)}, bf16[128,2048]{1,0:T(8,128)(2,1)S(1)}, u32[]{:S(2)}, u32[]{:S(2)}) collective-permute-start(bf16[128,2048]{1,0:T(8,128)(2,1)S(1)} %collective-permute-done.10.refs_4_), channel_id=1, source_target_pairs={{0,8},{4,12},{8,24},{12,28},{24,16},{28,20},{16,0},{20,4},{1,9},{5... | collective-permute-start | bytes 1572872 | tf_op jit(solution)/shard_map/ppermute | solution.py:554
  72.2 23.0 %collective-permute-start.13 = (bf16[2,64,2048]{2,1,0:T(8,128)(2,1)S(1)}, bf16[2,64,2048]{2,1,0:T(8,128)(2,1)S(1)}, u32[]{:S(2)}, u32[]{:S(2)}) collective-permute-start(bf16[2,64,2048]{2,1,0:T(8,128)(2,1)S(1)} %get-tuple-element.63), channel_id=1, source_target_pairs={{0,4},{1,5},{2,6},{3,7},{4,0},{5,1},{6,2},{7,3},{8,12},{9,13},{10,... | collective-permute-start | bytes 1572872 | tf_op jit(solution)/shard_map/ppermute | solution.py:563
  73.7 38.1 %collective-permute-start.17 = (bf16[64,2048]{1,0:T(8,128)(2,1)S(1)}, bf16[64,2048]{1,0:T(8,128)(2,1)S(1)}, u32[]{:S(2)}, u32[]{:S(2)}) collective-permute-start(bf16[64,2048]{1,0:T(8,128)(2,1)S(1)} %get-tuple-element.73.refs_2_.refs_11_), channel_id=1, source_target_pairs={{0,2},{1,3},{2,0},{3,1},{4,6},{5,7},{6,4},{7,5},{8,10},{9,11},{10,... | collective-permute-start | bytes 786440 | tf_op jit(solution)/shard_map/ppermute | solution.py:563
  74.8 37.1 %collective-permute-start.18 = (bf16[64,2048]{1,0:T(8,128)(2,1)S(1)}, bf16[64,2048]{1,0:T(8,128)(2,1)S(1)}, u32[]{:S(2)}, u32[]{:S(2)}) collective-permute-start(bf16[64,2048]{1,0:T(8,128)(2,1)S(1)} %get-tuple-element.77), channel_id=1, source_target_pairs={{0,6},{1,7},{2,4},{3,5},{4,2},{5,3},{6,0},{7,1},{8,14},{9,15},{10,... | collective-permute-start | bytes 786440 | tf_op jit(solution)/shard_map/ppermute | solution.py:563
  91.9 44.4 %collective-permute-start.19 = (bf16[1408,256]{1,0:T(8,128)(2,1)}, bf16[1408,256]{1,0:T(8,128)(2,1)}, u32[]{:S(2)}, u32[]{:S(2)}) collective-permute-start(bf16[1408,256]{1,0:T(8,128)(2,1)} %get-tuple-element.83), channel_id=1, source_target_pairs={{0,2},{1,3},{2,0},{3,1},{4,6},{5,7},{6,4},{7,5},{8,10},{9,11},{10,... | collective-permute-start | bytes 2162696 | tf_op jit(solution)/shard_map/ppermute | solution.py:563
  93.7 11.5 %collective-permute-start.16 = (bf16[64,2048]{1,0:T(8,128)(2,1)S(1)}, bf16[64,2048]{1,0:T(8,128)(2,1)S(1)}, u32[]{:S(2)}, u32[]{:S(2)}) collective-permute-start(bf16[64,2048]{1,0:T(8,128)(2,1)S(1)} %get-tuple-element.72.refs_5_), channel_id=1, source_target_pairs={{0,4},{1,5},{2,6},{3,7},{4,0},{5,1},{6,2},{7,3},{8,12},{9,13},{10,... | collective-permute-start | bytes 786440 | tf_op jit(solution)/shard_map/ppermute | solution.py:563
  111.4 20.6 %collective-permute-start.21 = (bf16[352,2048]{1,0:T(8,128)(2,1)}, bf16[352,2048]{1,0:T(8,128)(2,1)}, u32[]{:S(2)}, u32[]{:S(2)}) collective-permute-start(bf16[352,2048]{1,0:T(8,128)(2,1)} %get-tuple-element.86), channel_id=1, source_target_pairs={{0,1},{1,0},{2,3},{3,2},{4,5},{5,4},{6,7},{7,6},{8,9},{9,8},{10,11... | collective-permute-start | bytes 4325384 | tf_op jit(solution)/shard_map/ppermute | solution.py:563
  111.4 34.8 %collective-permute-start.22 = (bf16[352,2048]{1,0:T(8,128)(2,1)}, bf16[352,2048]{1,0:T(8,128)(2,1)}, u32[]{:S(2)}, u32[]{:S(2)}) collective-permute-start(bf16[352,2048]{1,0:T(8,128)(2,1)} %get-tuple-element.87), channel_id=1, source_target_pairs={{0,1},{1,0},{2,3},{3,2},{4,5},{5,4},{6,7},{7,6},{8,9},{9,8},{10,11... | collective-permute-start | bytes 4325384 | tf_op jit(solution)/shard_map/ppermute | solution.py:563
  126.8 19.3 %collective-permute-start.20 = (bf16[1408,256]{1,0:T(8,128)(2,1)}, bf16[1408,256]{1,0:T(8,128)(2,1)}, u32[]{:S(2)}, u32[]{:S(2)}) collective-permute-start(bf16[1408,256]{1,0:T(8,128)(2,1)} %get-tuple-element.84), channel_id=1, source_target_pairs={{0,2},{1,3},{2,0},{3,1},{4,6},{5,7},{6,4},{7,5},{8,10},{9,11},{10,... | collective-permute-start | bytes 2162696 | tf_op jit(solution)/shard_map/ppermute | solution.py:563
  127.3 55.5 %all-to-all-start = ((bf16[8,64,2048]{2,1,0:T(8,128)(2,1)}), bf16[8,64,2048]{2,1,0:T(8,128)(2,1)S(1)}, u32[]{:S(2)}, u32[]{:S(2)}) async-start(bf16[8,64,2048]{2,1,0:T(8,128)(2,1)} %copy-done.3), calls=%async_computation | async-start | bytes 4194304 | tf_op jit(solution)/shard_map/all_to_all | solution.py:623
  134.7 41.3 %collective-permute-start.24 = (bf16[352,2048]{1,0:T(8,128)(2,1)S(1)}, bf16[352,2048]{1,0:T(8,128)(2,1)S(1)}, u32[]{:S(2)}, u32[]{:S(2)}) collective-permute-start(bf16[352,2048]{1,0:T(8,128)(2,1)S(1)} %add_convert_fusion.refs_21_), channel_id=1, source_target_pairs={{0,2},{1,3},{2,0},{3,1},{4,6},{5,7},{6,4},{7,5},{8,10},{9,11},{10,... | collective-permute-start | bytes 4325384 | tf_op jit(solution)/shard_map/ppermute | solution.py:563
  158.9 21.0 %collective-permute-start.23 = (bf16[2,352,2048]{2,1,0:T(8,128)(2,1)}, bf16[2,352,2048]{2,1,0:T(8,128)(2,1)S(1)}, u32[]{:S(2)}, u32[]{:S(2)}) collective-permute-start(bf16[2,352,2048]{2,1,0:T(8,128)(2,1)} %get-tuple-element.89), channel_id=1, source_target_pairs={{0,1},{1,0},{2,3},{3,2},{4,5},{5,4},{6,7},{7,6},{8,9},{9,8},{10,11... | collective-permute-start | bytes 8650760 | tf_op jit(solution)/shard_map/ppermute | solution.py:563
  (45 other events, 582.4 us)

commit v2 on v1

--- a/solution.py
+++ b/solution.py
@@ -489,41 +489,65 @@
     )
 
 
-def sum_down_kernel(*refs):
-    total = refs[0][...].astype(F32)
-    for ref in refs[1:-1]:
-        total = total + ref[...].astype(F32)
-    refs[-1][...] = total.astype(BF16)
-
-
-def sum_down(order, terms):
-    return order.call(
-        sum_down_kernel,
-        [inside()] * len(terms),
-        terms,
-        cost=large_cost(),
+def arrive_kernel(*refs):
+    refs[-1][...] = jnp.zeros_like(refs[-1])
+
+
+def arrive(order, value):
+    return order.call(
+        arrive_kernel,
+        [],
+        [],
+        [value],
+        large_cost(),
         out_specs=inside(),
-        out_shape=jax.ShapeDtypeStruct(terms[0].shape, BF16),
-        name="sum_down",
-    )
-
-
-def sum_kernel(keep_ref, come_ref, down_ref, out_ref):
+        out_shape=jax.ShapeDtypeStruct((8, 128), F32),
+        name="arrive",
+    )
+
+
+def sum_kernel(keep_ref, come_ref, *refs):
+    down_refs, (out_ref, downs, total, sems, out_sems) = refs[:-5], refs[-5:]
     width = keep_ref.shape[2]
-    for lead in range(2):
-        total = keep_ref[lead].astype(F32) + come_ref[lead].astype(F32)
-        out_ref[:, lead * width : (lead + 1) * width] = total.astype(BF16)
-    out_ref[:, 2 * width :] = down_ref[...]
-
-
-def sum_all(order, keep, come, down):
+    copies = [
+        pltpu.make_async_copy(ref, downs.at[i], sems.at[i]) for i, ref in enumerate(down_refs)
+    ]
+    for copy in copies:
+        copy.start()
+    outs = []
+    for part in range(3):
+        columns = pl.ds(part * width, width)
+        if part < 2:
+            value = keep_ref[part].astype(F32) + come_ref[part].astype(F32)
+        else:
+            for copy in copies:
+                copy.wait()
+            value = downs[0].astype(F32)
+            for i in range(1, len(down_refs)):
+                value = value + downs[i].astype(F32)
+        total[part] = value.astype(BF16)
+        outs.append(
+            pltpu.make_async_copy(total.at[part], out_ref.at[:, columns], out_sems.at[part])
+        )
+        outs[-1].start()
+    for copy in outs:
+        copy.wait()
+
+
+def sum_all(order, keep, come, downs):
     _, own, width = keep.shape
     return order.call(
         sum_kernel,
-        [inside()] * 3,
-        [keep, come, down],
-        out_specs=inside(),
+        [inside()] * 2 + [anywhere()] * len(downs),
+        [keep, come, *downs],
+        out_specs=anywhere(),
         out_shape=jax.ShapeDtypeStruct((own, 3 * width), BF16),
+        scratch_shapes=[
+            pltpu.VMEM((len(downs), own, width), BF16),
+            pltpu.VMEM((3, own, width), BF16),
+            pltpu.SemaphoreType.DMA((len(downs),)),
+            pltpu.SemaphoreType.DMA((3,)),
+        ],
         name="sum_all",
     )
 
@@ -586,11 +610,11 @@
             2: [value for value, _ in x_other[columns:]],
             3: [value for value, _ in x_other[2 * columns :]],
         }[s]
-        d_next = along_ring(d_block) if s > 1 else None
+        d_next = along_ring(d_block) if s > 2 else None
         keep_x, keep_d, pairs, sends, again, scales, hits = select_both(
-            order, place, x_block, scales, hits, d_block, columns, s == 1, waits
+            order, place, x_block, scales, hits, d_block, columns, s < 3, waits
         )
-        if s == 1:
+        if s < 3:
             d_next = along_ring(again)
         come = exchange(pairs, 0)
         x_pieces += [(keep_x, None)] + [(value, 0) for value in come]
@@ -629,8 +653,8 @@
     send, keep = grad_x(
         order, place, acts_kept + acts_come, x_pieces + x_other, width, [summed, down_core]
     )
-    down = sum_down(order, [down_own, down_core, down_y])
-    g_rows = sum_all(order, keep, across(send, 0, 1), down)
+    arrive(order, down_y)
+    g_rows = sum_all(order, keep, across(send, 0, 1), [down_own, down_core, down_y])
     d_tokens = merge(order, all_hits, returned.reshape(experts * capacity, width))
     return d_tokens, g_rows[None]
 

time: 187 us -> 184 us (0.984)
  waiting for transfers between devices: 63.9 us -> 58.8 us
  local copies, waits for them, and re-layouts: 13.1 us -> 15.1 us
    ppermute x19, waiting for transfers between devices: 31.1 us -> 28.1 us  [across(): return lax.ppermute(value, ('expert', 'replica'), pairs)]
    ppermute x6, waiting for transfers between devices: 32.8 us -> 30.7 us  [along_ring(): return lax.ppermute(value, 'expert', pairs)]
    unnamed x86, local copies, waits for them, and re-layouts: 13 us -> 15 us
    ppermute x6, starting transfers between devices: 9.52 us -> 11.5 us  [along_ring(): return lax.ppermute(value, 'expert', pairs)]
  transfers between devices with their start and end apart: 26 -> 26, of which waited for: 8 -> 7; matrix products, arithmetic and copies ran while one was open for 1% -> 1% of each run, Pallas kernels for 36% -> 36%
where the time goes in v2:
time: 184 us; the launch traced here: 183 us
  Pallas kernels  67.5 us (37%)
  waiting for transfers between devices  58.8 us (32%)
  starting transfers between devices  36 us (20%)
  local copies, waits for them, and re-layouts  15.1 us (8%)
  other arithmetic  3.95 us (2%)
    pallas_call x15, Pallas kernels, call(): pl.pallas_call(body_of, in_specs=list(specs) + [anywhere()] * len(extra),...  67.5 us
    ppermute x6, waiting for transfers between devices, along_ring(): return lax.ppermute(value, 'expert', pairs)  30.7 us
    ppermute x19, waiting for transfers between devices, across(): return lax.ppermute(value, ('expert', 'replica'), pairs)  28.1 us
    ppermute x19, starting transfers between devices, across(): return lax.ppermute(value, ('expert', 'replica'), pairs)  19.9 us
    unnamed x86, local copies, waits for them, and re-layouts  15 us
    ppermute x6, starting transfers between devices, along_ring(): return lax.ppermute(value, 'expert', pairs)  11.5 us
    all_to_all x1, starting transfers between devices, body(): lax.all_to_all(dx, 'expert', split_axis=0, concat_axis=0, tiled=True)  4.66 us
  transfers between devices with their start and end apart: 26, of which 7 were waited for; matrix products, arithmetic and copies ran while one was open for 1% of the time, Pallas kernels for 36%

profile of v2, /device:TPU:0, one launch (start us, length us, event | category | flops | bytes accessed | tf_op | source)
XLA Modules:
  0.0 182.8 jit_solution(3849537547868595254)
XLA Ops:
  4.1 3.1 %collective-permute-start = (bf16[128,2176]{1,0:T(8,128)(2,1)S(1)}, bf16[128,2176]{1,0:T(8,128)(2,1)S(1)}, u32[]{:S(2)}, u32[]{:S(2)}) collective-permute-start(bf16[128,2176]{1,0:T(8,128)(2,1)S(1)} %get-tuple-element.48), channel_id=1, source_target_pairs={{0,8},{4,12},{8,24},{12,28},{24,16},{28,20},{16,0},{20,4},{1,9},{5... | collective-permute-start | bytes 1671176 | tf_op jit(solution)/shard_map/ppermute | solution.py:578
  10.7 10.2 %collective-permute-done.refs_1_ = bf16[128,2176]{1,0:T(8,128)(2,1)S(1)} collective-permute-done((bf16[128,2176]{1,0:T(8,128)(2,1)S(1)}, bf16[128,2176]{1,0:T(8,128)(2,1)S(1)}, u32[]{:S(2)}, u32[]{:S(2)}) %collective-permute-start) | collective-permute-done | bytes 557088 | tf_op jit(solution)/shard_map/ppermute | solution.py:578
  24.3 1.6 collective-permute-start.9
  25.9 3.4 %collective-permute-start.6 = (bf16[128,2048]{1,0:T(8,128)(2,1)S(1)}, bf16[128,2048]{1,0:T(8,128)(2,1)S(1)}, u32[]{:S(2)}, u32[]{:S(2)}) collective-permute-start(bf16[128,2048]{1,0:T(8,128)(2,1)S(1)} %get-tuple-element.54), channel_id=1, source_target_pairs={{0,8},{4,12},{8,24},{12,28},{24,16},{28,20},{16,0},{20,4},{1,9},{5... | collective-permute-start | bytes 1572872 | tf_op jit(solution)/shard_map/ppermute | solution.py:578
  31.2 6.1 %collective-permute-done.1.refs_1_ = bf16[128,2176]{1,0:T(8,128)(2,1)S(1)} collective-permute-done((bf16[128,2176]{1,0:T(8,128)(2,1)S(1)}, bf16[128,2176]{1,0:T(8,128)(2,1)S(1)}, u32[]{:S(2)}, u32[]{:S(2)}) %collective-permute-start.1) | collective-permute-done | bytes 557088 | tf_op jit(solution)/shard_map/ppermute | solution.py:578
  39.2 8.6 %gate_up.2 = (bf16[2,704,256]{2,1,0:T(8,128)(2,1)S(1)}, f32[2,704,256]{2,1,0:T(8,128)S(1)}, f32[2,704,256]{2,1,0:T(8,128)S(1)}) custom-call(bf16[64,2048]{1,0:T(8,128)(2,1)S(1)} %get-tuple-element.51.refs_0_.refs_5_, bf16[64,2048]{1,0:T(8,128)(2,1)S(1)} %collective-permute-done.3.refs_5_.refs_1_.refs_6_, ...), custom_call_target="tpu_custom_call" | custom-call | flops 1024 | bytes 1024 | tf_op jit(solution)/shard_map/gate_up/pallas_call | solution.py:55
  49.7 2.9 %collective-permute-start.10 = (bf16[128,2048]{1,0:T(8,128)(2,1)S(1)}, bf16[128,2048]{1,0:T(8,128)(2,1)S(1)}, u32[]{:S(2)}, u32[]{:S(2)}) collective-permute-start(bf16[128,2048]{1,0:T(8,128)(2,1)S(1)} %get-tuple-element.61), channel_id=1, source_target_pairs={{0,8},{4,12},{8,24},{12,28},{24,16},{28,20},{16,0},{20,4},{1,9},{5... | collective-permute-start | bytes 1572872 | tf_op jit(solution)/shard_map/ppermute | solution.py:578
  56.1 13.9 %collective-permute-done.10.refs_4_ = bf16[128,2048]{1,0:T(8,128)(2,1)S(1)} collective-permute-done((bf16[128,2048]{1,0:T(8,128)(2,1)S(1)}, bf16[128,2048]{1,0:T(8,128)(2,1)S(1)}, u32[]{:S(2)}, u32[]{:S(2)}) %collective-permute-start.10) | collective-permute-done | bytes 524320 | tf_op jit(solution)/shard_map/ppermute | solution.py:578
  71.7 1.6 collective-permute-start.13
  75.3 12.5 %backward.2 = (bf16[8,64,2048]{2,1,0:T(8,128)(2,1)S(1)}, bf16[1408,256]{1,0:T(8,128)(2,1)}, bf16[1408,256]{1,0:T(8,128)(2,1)S(1)}) custom-call(s32[8]{0:T(128)S(1)} %stack.35.refs_0_, bf16[64,2048]{1,0:T(8,128)(2,1)S(1)} %get-tuple-element.68.refs_1_.refs_3_, bf16[2,64,2048]{2,1,0:T(8,128)(2,1)S(1)} %collective-permute-done.9.refs_3_.refs_2_.refs_4_.refs_8_, ...), custom_call_target="tpu_custom_call" | custom-call | flops 1024 | bytes 1024 | tf_op jit(solution)/shard_map/backward/pallas_call | solution.py:55
  87.7 1.6 collective-permute-start.19
  91.2 8.9 %gate_up.3 = (bf16[2,704,256]{2,1,0:T(8,128)(2,1)S(1)}, f32[2,704,256]{2,1,0:T(8,128)S(1)}, f32[2,704,256]{2,1,0:T(8,128)S(1)}) custom-call(bf16[64,2048]{1,0:T(8,128)(2,1)S(1)} %get-tuple-element.62.refs_0_.refs_9_, bf16[2,64,2048]{2,1,0:T(8,128)(2,1)S(1)} %collective-permute-done.15.refs_4_.refs_1_.refs_6_.refs_10_, ...), custom_call_target="tpu_custom_call" | custom-call | flops 40000000000 | bytes 134217728 | tf_op jit(solution)/shard_map/gate_up/pallas_call | solution.py:55
  101.2 5.0 %grad_down.1 = (bf16[352,2048]{1,0:T(8,128)(2,1)}, bf16[352,2048]{1,0:T(8,128)(2,1)S(1)}, bf16[352,2048]{1,0:T(8,128)(2,1)}, bf16[352,2048]{1,0:T(8,128)(2,1)S(1)}) custom-call(s32[8]{0:T(128)S(1)} %stack.35.refs_0_, bf16[2,704,256]{2,1,0:T(8,128)(2,1)S(1)} %get-tuple-element.80.refs_1_, bf16[2,704,256]{2,1,0:T(8,128)(2,1)S(1)} %get-tuple-element.81.refs_2_, ...), custom_call_target="tpu_custom_call" | custom-call | flops 1024 | bytes 1024 | tf_op jit(solution)/shard_map/grad_down/pallas_call | solution.py:55
  107.9 12.7 %backward.3 = (bf16[8,64,2048]{2,1,0:T(8,128)(2,1)S(1)}, bf16[1408,256]{1,0:T(8,128)(2,1)}, bf16[1408,256]{1,0:T(8,128)(2,1)S(1)}) custom-call(s32[8]{0:T(128)S(1)} %stack.35.refs_0_, bf16[64,2048]{1,0:T(8,128)(2,1)S(1)} %get-tuple-element.64.refs_7_.refs_1_, ...), custom_call_target="tpu_custom_call", output_to_operand_aliasing={{0}: (8, {})} | custom-call | flops 40000000000 | bytes 134217728 | tf_op jit(solution)/shard_map/backward/pallas_call | solution.py:55
  123.3 4.7 %all-to-all-start = ((bf16[8,64,2048]{2,1,0:T(8,128)(2,1)}), bf16[8,64,2048]{2,1,0:T(8,128)(2,1)S(1)}, u32[]{:S(2)}, u32[]{:S(2)}) async-start(bf16[8,64,2048]{2,1,0:T(8,128)(2,1)} %copy-done.3), calls=%async_computation | async-start | bytes 4194304 | tf_op jit(solution)/shard_map/all_to_all | solution.py:647
  128.1 2.6 %add_convert_fusion.refs_21_ = bf16[352,2048]{1,0:T(8,128)(2,1)S(1)} fusion(bf16[352,2048]{1,0:T(8,128)(2,1)} %collective-permute-done.21, bf16[352,2048]{1,0:T(8,128)(2,1)} %copy-done.4), kind=kLoop, calls=%fused_computation | loop fusion | flops 2883584 | bytes 4325376 | tf_op jit(solution)/shard_map/convert_element_type | solution.py:649
  130.7 1.6 collective-permute-start.24
  132.3 9.8 %collective-permute-done.20.refs_4_ = bf16[1408,256]{1,0:T(8,128)(2,1)} collective-permute-done((bf16[1408,256]{1,0:T(8,128)(2,1)}, bf16[1408,256]{1,0:T(8,128)(2,1)}, u32[]{:S(2)}, u32[]{:S(2)}) %collective-permute-start.20) | collective-permute-done | bytes 720928 | tf_op jit(solution)/shard_map/ppermute | solution.py:587
  144.3 10.4 %grad_x.1 = (bf16[2,352,2048]{2,1,0:T(8,128)(2,1)}, bf16[2,352,2048]{2,1,0:T(8,128)(2,1)}) custom-call(s32[8]{0:T(128)S(1)} %stack.35.refs_0_, bf16[1408,256]{1,0:T(8,128)(2,1)S(1)} %copy-done.12, bf16[1408,256]{1,0:T(8,128)(2,1)S(1)} %copy-done.42, bf16[1408,256]{1,0:T(8,128)(2,1)} %collective-permute-done.19.refs_3_, ...), custom_call_target="tpu_custom_call" | custom-call | flops 40000000000 | bytes 134217728 | tf_op jit(solution)/shard_map/grad_x/pallas_call | solution.py:55
  154.8 17.1 %collective-permute-done.24.refs_0_.refs_4_ = bf16[352,2048]{1,0:T(8,128)(2,1)S(1)} collective-permute-done((bf16[352,2048]{1,0:T(8,128)(2,1)S(1)}, bf16[352,2048]{1,0:T(8,128)(2,1)S(1)}, u32[]{:S(2)}, u32[]{:S(2)}) %collective-permute-start.24) | collective-permute-done | bytes 1441824 | tf_op jit(solution)/shard_map/ppermute | solution.py:587
  172.0 1.8 copy-done.1
  173.8 1.8 copy-done.2
  176.0 3.3 %sum_all.1.refs_2_ = bf16[352,6144]{1,0:T(8,128)(2,1)} custom-call(bf16[2,352,2048]{2,1,0:T(8,128)(2,1)S(1)} %copy-done.2, bf16[2,352,2048]{2,1,0:T(8,128)(2,1)S(1)} %collective-permute-done.23.refs_1_, bf16[352,2048]{1,0:T(8,128)(2,1)S(1)} %copy-done.6, bf16[352,2048]{1,0:T(8,128)(2,1)} %collective-permute-done.22.refs_22_.refs_3_, ...), custom_call_target="tpu_custom_call" | custom-call | flops 1024 | bytes 1024 | tf_op jit(solution)/shard_map/sum_all/pallas_call | solution.py:55
  179.3 2.2 %copy-done = bf16[352,6144]{1,0:T(8,128)(2,1)S(1)} copy-done((bf16[352,6144]{1,0:T(8,128)(2,1)S(1)}, bf16[352,6144]{1,0:T(8,128)(2,1)}, u32[]{:S(2)}) %copy-start) | copy-done | bytes 4325400
  (133 shorter events, 34.3 us)
Async XLA Ops:
  4.1 16.7 %collective-permute-start = (bf16[128,2176]{1,0:T(8,128)(2,1)S(1)}, bf16[128,2176]{1,0:T(8,128)(2,1)S(1)}, u32[]{:S(2)}, u32[]{:S(2)}) collective-permute-start(bf16[128,2176]{1,0:T(8,128)(2,1)S(1)} %get-tuple-element.48), channel_id=1, source_target_pairs={{0,8},{4,12},{8,24},{12,28},{24,16},{28,20},{16,0},{20,4},{1,9},{5... | collective-permute-start | bytes 1671176 | tf_op jit(solution)/shard_map/ppermute | solution.py:578
  7.2 14.7 %collective-permute-start.3 = (bf16[64,2048]{1,0:T(8,128)(2,1)S(1)}, bf16[64,2048]{1,0:T(8,128)(2,1)S(1)}, u32[]{:S(2)}, u32[]{:S(2)}) collective-permute-start(bf16[64,2048]{1,0:T(8,128)(2,1)S(1)} %get-tuple-element.50), channel_id=1, source_target_pairs={{0,4},{1,5},{2,6},{3,7},{4,0},{5,1},{6,2},{7,3},{8,12},{9,13},{10,... | collective-permute-start | bytes 786440 | tf_op jit(solution)/shard_map/ppermute | solution.py:587
  8.7 13.2 %collective-permute-start.4 = (bf16[64,2048]{1,0:T(8,128)(2,1)S(1)}, bf16[64,2048]{1,0:T(8,128)(2,1)S(1)}, u32[]{:S(2)}, u32[]{:S(2)}) collective-permute-start(bf16[64,2048]{1,0:T(8,128)(2,1)S(1)} %get-tuple-element.51.refs_0_.refs_5_), channel_id=1, source_target_pairs={{0,2},{1,3},{2,0},{3,1},{4,6},{5,7},{6,4},{7,5},{8,10},{9,11},{10,... | collective-permute-start | bytes 786440 | tf_op jit(solution)/shard_map/ppermute | solution.py:587
  20.9 16.5 %collective-permute-start.1 = (bf16[128,2176]{1,0:T(8,128)(2,1)S(1)}, bf16[128,2176]{1,0:T(8,128)(2,1)S(1)}, u32[]{:S(2)}, u32[]{:S(2)}) collective-permute-start(bf16[128,2176]{1,0:T(8,128)(2,1)S(1)} %collective-permute-done.refs_1_), channel_id=1, source_target_pairs={{0,8},{4,12},{8,24},{12,28},{24,16},{28,20},{16,0},{20,4},{1,9},{5... | collective-permute-start | bytes 1671176 | tf_op jit(solution)/shard_map/ppermute | solution.py:578
  24.3 14.9 %collective-permute-start.9 = (bf16[2,64,2048]{2,1,0:T(8,128)(2,1)S(1)}, bf16[2,64,2048]{2,1,0:T(8,128)(2,1)S(1)}, u32[]{:S(2)}, u32[]{:S(2)}) collective-permute-start(bf16[2,64,2048]{2,1,0:T(8,128)(2,1)S(1)} %get-tuple-element.57), channel_id=1, source_target_pairs={{0,4},{1,5},{2,6},{3,7},{4,0},{5,1},{6,2},{7,3},{8,12},{9,13},{10,... | collective-permute-start | bytes 1572872 | tf_op jit(solution)/shard_map/ppermute | solution.py:587
  25.9 22.7 %collective-permute-start.6 = (bf16[128,2048]{1,0:T(8,128)(2,1)S(1)}, bf16[128,2048]{1,0:T(8,128)(2,1)S(1)}, u32[]{:S(2)}, u32[]{:S(2)}) collective-permute-start(bf16[128,2048]{1,0:T(8,128)(2,1)S(1)} %get-tuple-element.54), channel_id=1, source_target_pairs={{0,8},{4,12},{8,24},{12,28},{24,16},{28,20},{16,0},{20,4},{1,9},{5... | collective-permute-start | bytes 1572872 | tf_op jit(solution)/shard_map/ppermute | solution.py:578
  29.2 18.7 %collective-permute-start.7 = (bf16[64,2048]{1,0:T(8,128)(2,1)S(1)}, bf16[64,2048]{1,0:T(8,128)(2,1)S(1)}, u32[]{:S(2)}, u32[]{:S(2)}) collective-permute-start(bf16[64,2048]{1,0:T(8,128)(2,1)S(1)} %get-tuple-element.55.refs_2_.refs_7_), channel_id=1, source_target_pairs={{0,2},{1,3},{2,0},{3,1},{4,6},{5,7},{6,4},{7,5},{8,10},{9,11},{10,... | collective-permute-start | bytes 786440 | tf_op jit(solution)/shard_map/ppermute | solution.py:587
  30.8 17.2 %collective-permute-start.8 = (bf16[64,2048]{1,0:T(8,128)(2,1)S(1)}, bf16[64,2048]{1,0:T(8,128)(2,1)S(1)}, u32[]{:S(2)}, u32[]{:S(2)}) collective-permute-start(bf16[64,2048]{1,0:T(8,128)(2,1)S(1)} %get-tuple-element.56), channel_id=1, source_target_pairs={{0,6},{1,7},{2,4},{3,5},{4,2},{5,3},{6,0},{7,1},{8,14},{9,15},{10,... | collective-permute-start | bytes 786440 | tf_op jit(solution)/shard_map/ppermute | solution.py:587
  37.3 33.2 %collective-permute-start.2 = (bf16[128,2176]{1,0:T(8,128)(2,1)S(1)}, bf16[128,2176]{1,0:T(8,128)(2,1)S(1)}, u32[]{:S(2)}, u32[]{:S(2)}) collective-permute-start(bf16[128,2176]{1,0:T(8,128)(2,1)S(1)} %collective-permute-done.1.refs_1_), channel_id=1, source_target_pairs={{0,8},{4,12},{8,24},{12,28},{24,16},{28,20},{16,0},{20,4},{1,9},{5... | collective-permute-start | bytes 1671176 | tf_op jit(solution)/shard_map/ppermute | solution.py:578
  49.7 20.2 %collective-permute-start.10 = (bf16[128,2048]{1,0:T(8,128)(2,1)S(1)}, bf16[128,2048]{1,0:T(8,128)(2,1)S(1)}, u32[]{:S(2)}, u32[]{:S(2)}) collective-permute-start(bf16[128,2048]{1,0:T(8,128)(2,1)S(1)} %get-tuple-element.61), channel_id=1, source_target_pairs={{0,8},{4,12},{8,24},{12,28},{24,16},{28,20},{16,0},{20,4},{1,9},{5... | collective-permute-start | bytes 1572872 | tf_op jit(solution)/shard_map/ppermute | solution.py:578
  52.6 17.9 %collective-permute-start.11 = (bf16[64,2048]{1,0:T(8,128)(2,1)S(1)}, bf16[64,2048]{1,0:T(8,128)(2,1)S(1)}, u32[]{:S(2)}, u32[]{:S(2)}) collective-permute-start(bf16[64,2048]{1,0:T(8,128)(2,1)S(1)} %get-tuple-element.62.refs_0_.refs_9_), channel_id=1, source_target_pairs={{0,2},{1,3},{2,0},{3,1},{4,6},{5,7},{6,4},{7,5},{8,10},{9,11},{10,... | collective-permute-start | bytes 786440 | tf_op jit(solution)/shard_map/ppermute | solution.py:587
  54.1 16.4 %collective-permute-start.12 = (bf16[64,2048]{1,0:T(8,128)(2,1)S(1)}, bf16[64,2048]{1,0:T(8,128)(2,1)S(1)}, u32[]{:S(2)}, u32[]{:S(2)}) collective-permute-start(bf16[64,2048]{1,0:T(8,128)(2,1)S(1)} %get-tuple-element.63), channel_id=1, source_target_pairs={{0,6},{1,7},{2,4},{3,5},{4,2},{5,3},{6,0},{7,1},{8,14},{9,15},{10,... | collective-permute-start | bytes 786440 | tf_op jit(solution)/shard_map/ppermute | solution.py:587
  55.5 19.7 %collective-permute-start.15 = (bf16[2,64,2048]{2,1,0:T(8,128)(2,1)S(1)}, bf16[2,64,2048]{2,1,0:T(8,128)(2,1)S(1)}, u32[]{:S(2)}, u32[]{:S(2)}) collective-permute-start(bf16[2,64,2048]{2,1,0:T(8,128)(2,1)S(1)} %get-tuple-element.70), channel_id=1, source_target_pairs={{0,4},{1,5},{2,6},{3,7},{4,0},{5,1},{6,2},{7,3},{8,12},{9,13},{10,... | collective-permute-start | bytes 1572872 | tf_op jit(solution)/shard_map/ppermute | solution.py:587
  70.0 19.4 %collective-permute-start.14 = (bf16[128,2048]{1,0:T(8,128)(2,1)S(1)}, bf16[128,2048]{1,0:T(8,128)(2,1)S(1)}, u32[]{:S(2)}, u32[]{:S(2)}) collective-permute-start(bf16[128,2048]{1,0:T(8,128)(2,1)S(1)} %collective-permute-done.10.refs_4_), channel_id=1, source_target_pairs={{0,8},{4,12},{8,24},{12,28},{24,16},{28,20},{16,0},{20,4},{1,9},{5... | collective-permute-start | bytes 1572872 | tf_op jit(solution)/shard_map/ppermute | solution.py:578
  71.7 19.5 %collective-permute-start.13 = (bf16[2,64,2048]{2,1,0:T(8,128)(2,1)S(1)}, bf16[2,64,2048]{2,1,0:T(8,128)(2,1)S(1)}, u32[]{:S(2)}, u32[]{:S(2)}) collective-permute-start(bf16[2,64,2048]{2,1,0:T(8,128)(2,1)S(1)} %get-tuple-element.65), channel_id=1, source_target_pairs={{0,4},{1,5},{2,6},{3,7},{4,0},{5,1},{6,2},{7,3},{8,12},{9,13},{10,... | collective-permute-start | bytes 1572872 | tf_op jit(solution)/shard_map/ppermute | solution.py:587
  73.2 34.6 %collective-permute-start.17 = (bf16[64,2048]{1,0:T(8,128)(2,1)S(1)}, bf16[64,2048]{1,0:T(8,128)(2,1)S(1)}, u32[]{:S(2)}, u32[]{:S(2)}) collective-permute-start(bf16[64,2048]{1,0:T(8,128)(2,1)S(1)} %get-tuple-element.75.refs_2_.refs_11_), channel_id=1, source_target_pairs={{0,2},{1,3},{2,0},{3,1},{4,6},{5,7},{6,4},{7,5},{8,10},{9,11},{10,... | collective-permute-start | bytes 786440 | tf_op jit(solution)/shard_map/ppermute | solution.py:587
  74.8 33.1 %collective-permute-start.18 = (bf16[64,2048]{1,0:T(8,128)(2,1)S(1)}, bf16[64,2048]{1,0:T(8,128)(2,1)S(1)}, u32[]{:S(2)}, u32[]{:S(2)}) collective-permute-start(bf16[64,2048]{1,0:T(8,128)(2,1)S(1)} %get-tuple-element.79), channel_id=1, source_target_pairs={{0,6},{1,7},{2,4},{3,5},{4,2},{5,3},{6,0},{7,1},{8,14},{9,15},{10,... | collective-permute-start | bytes 786440 | tf_op jit(solution)/shard_map/ppermute | solution.py:587
  87.7 44.5 %collective-permute-start.19 = (bf16[1408,256]{1,0:T(8,128)(2,1)}, bf16[1408,256]{1,0:T(8,128)(2,1)}, u32[]{:S(2)}, u32[]{:S(2)}) collective-permute-start(bf16[1408,256]{1,0:T(8,128)(2,1)} %get-tuple-element.85), channel_id=1, source_target_pairs={{0,2},{1,3},{2,0},{3,1},{4,6},{5,7},{6,4},{7,5},{8,10},{9,11},{10,... | collective-permute-start | bytes 2162696 | tf_op jit(solution)/shard_map/ppermute | solution.py:587
  107.3 20.6 %collective-permute-start.21 = (bf16[352,2048]{1,0:T(8,128)(2,1)}, bf16[352,2048]{1,0:T(8,128)(2,1)}, u32[]{:S(2)}, u32[]{:S(2)}) collective-permute-start(bf16[352,2048]{1,0:T(8,128)(2,1)} %get-tuple-element.88), channel_id=1, source_target_pairs={{0,1},{1,0},{2,3},{3,2},{4,5},{5,4},{6,7},{7,6},{8,9},{9,8},{10,11... | collective-permute-start | bytes 4325384 | tf_op jit(solution)/shard_map/ppermute | solution.py:587
  107.3 34.8 %collective-permute-start.22 = (bf16[352,2048]{1,0:T(8,128)(2,1)}, bf16[352,2048]{1,0:T(8,128)(2,1)}, u32[]{:S(2)}, u32[]{:S(2)}) collective-permute-start(bf16[352,2048]{1,0:T(8,128)(2,1)} %get-tuple-element.89), channel_id=1, source_target_pairs={{0,1},{1,0},{2,3},{3,2},{4,5},{5,4},{6,7},{7,6},{8,9},{9,8},{10,11... | collective-permute-start | bytes 4325384 | tf_op jit(solution)/shard_map/ppermute | solution.py:587
  122.8 19.3 %collective-permute-start.20 = (bf16[1408,256]{1,0:T(8,128)(2,1)}, bf16[1408,256]{1,0:T(8,128)(2,1)}, u32[]{:S(2)}, u32[]{:S(2)}) collective-permute-start(bf16[1408,256]{1,0:T(8,128)(2,1)} %get-tuple-element.86), channel_id=1, source_target_pairs={{0,2},{1,3},{2,0},{3,1},{4,6},{5,7},{6,4},{7,5},{8,10},{9,11},{10,... | collective-permute-start | bytes 2162696 | tf_op jit(solution)/shard_map/ppermute | solution.py:587
  123.3 56.0 %all-to-all-start = ((bf16[8,64,2048]{2,1,0:T(8,128)(2,1)}), bf16[8,64,2048]{2,1,0:T(8,128)(2,1)S(1)}, u32[]{:S(2)}, u32[]{:S(2)}) async-start(bf16[8,64,2048]{2,1,0:T(8,128)(2,1)} %copy-done.3), calls=%async_computation | async-start | bytes 4194304 | tf_op jit(solution)/shard_map/all_to_all | solution.py:647
  130.7 41.3 %collective-permute-start.24 = (bf16[352,2048]{1,0:T(8,128)(2,1)S(1)}, bf16[352,2048]{1,0:T(8,128)(2,1)S(1)}, u32[]{:S(2)}, u32[]{:S(2)}) collective-permute-start(bf16[352,2048]{1,0:T(8,128)(2,1)S(1)} %add_convert_fusion.refs_21_), channel_id=1, source_target_pairs={{0,2},{1,3},{2,0},{3,1},{4,6},{5,7},{6,4},{7,5},{8,10},{9,11},{10,... | collective-permute-start | bytes 4325384 | tf_op jit(solution)/shard_map/ppermute | solution.py:587
  154.7 19.0 %collective-permute-start.23 = (bf16[2,352,2048]{2,1,0:T(8,128)(2,1)}, bf16[2,352,2048]{2,1,0:T(8,128)(2,1)S(1)}, u32[]{:S(2)}, u32[]{:S(2)}) collective-permute-start(bf16[2,352,2048]{2,1,0:T(8,128)(2,1)} %get-tuple-element.91), channel_id=1, source_target_pairs={{0,1},{1,0},{2,3},{3,2},{4,5},{5,4},{6,7},{7,6},{8,9},{9,8},{10,11... | collective-permute-start | bytes 8650760 | tf_op jit(solution)/shard_map/ppermute | solution.py:587
  (45 other events, 505.7 us)

commit v3 on v2

--- a/solution.py
+++ b/solution.py
@@ -653,9 +653,9 @@
     send, keep = grad_x(
         order, place, acts_kept + acts_come, x_pieces + x_other, width, [summed, down_core]
     )
+    d_tokens = merge(order, all_hits, returned.reshape(experts * capacity, width))
     arrive(order, down_y)
     g_rows = sum_all(order, keep, across(send, 0, 1), [down_own, down_core, down_y])
-    d_tokens = merge(order, all_hits, returned.reshape(experts * capacity, width))
     return d_tokens, g_rows[None]
 
 

time: 184 us -> 190 us (1.033)
  Pallas kernels: 67.5 us -> 70.8 us
  waiting for transfers between devices: 58.8 us -> 62 us
    all_to_all x1, waiting for transfers between devices: 0.01 us -> 21.3 us  [body(): lax.all_to_all(dx, 'expert', split_axis=0, concat_axis=0, tiled=True)]
    ppermute x19, waiting for transfers between devices: 28.1 us -> 9.95 us  [across(): return lax.ppermute(value, ('expert', 'replica'), pairs)]
    pallas_call x15, Pallas kernels: 67.5 us -> 70.8 us  [call(): pl.pallas_call(body_of, in_specs=list(specs) + [anywhere()] * len(extra),...]
    unnamed x86 -> x82, local copies, waits for them, and re-layouts: 15 us -> 13.8 us
  transfers between devices with their start and end apart: 26 -> 26, of which waited for: 7 -> 7; matrix products, arithmetic and copies ran while one was open for 1% -> 2% of each run, Pallas kernels for 36% -> 33%
where the time goes in v3:
time: 190 us; the launch traced here: 189 us
  Pallas kernels  70.8 us (37%)
  waiting for transfers between devices  62 us (33%)
  starting transfers between devices  36 us (19%)
  local copies, waits for them, and re-layouts  13.9 us (7%)
  other arithmetic  5.02 us (3%)
    pallas_call x15, Pallas kernels, call(): pl.pallas_call(body_of, in_specs=list(specs) + [anywhere()] * len(extra),...  70.8 us
    ppermute x6, waiting for transfers between devices, along_ring(): return lax.ppermute(value, 'expert', pairs)  30.8 us
    all_to_all x1, waiting for transfers between devices, body(): lax.all_to_all(dx, 'expert', split_axis=0, concat_axis=0, tiled=True)  21.3 us
    ppermute x19, starting transfers between devices, across(): return lax.ppermute(value, ('expert', 'replica'), pairs)  19.8 us
    unnamed x82, local copies, waits for them, and re-layouts  13.8 us
    ppermute x6, starting transfers between devices, along_ring(): return lax.ppermute(value, 'expert', pairs)  11.5 us
    ppermute x19, waiting for transfers between devices, across(): return lax.ppermute(value, ('expert', 'replica'), pairs)  9.95 us
    all_to_all x1, starting transfers between devices, body(): lax.all_to_all(dx, 'expert', split_axis=0, concat_axis=0, tiled=True)  4.66 us
  transfers between devices with their start and end apart: 26, of which 7 were waited for; matrix products, arithmetic and copies ran while one was open for 2% of the time, Pallas kernels for 33%

profile of v3, /device:TPU:0, one launch (start us, length us, event | category | flops | bytes accessed | tf_op | source)
XLA Modules:
  0.0 189.2 jit_solution(14024900565028490680)
XLA Ops:
  4.1 3.1 %collective-permute-start = (bf16[128,2176]{1,0:T(8,128)(2,1)S(1)}, bf16[128,2176]{1,0:T(8,128)(2,1)S(1)}, u32[]{:S(2)}, u32[]{:S(2)}) collective-permute-start(bf16[128,2176]{1,0:T(8,128)(2,1)S(1)} %get-tuple-element.48), channel_id=1, source_target_pairs={{0,8},{4,12},{8,24},{12,28},{24,16},{28,20},{16,0},{20,4},{1,9},{5... | collective-permute-start | bytes 1671176 | tf_op jit(solution)/shard_map/ppermute | solution.py:578
  10.7 10.2 %collective-permute-done.refs_1_ = bf16[128,2176]{1,0:T(8,128)(2,1)S(1)} collective-permute-done((bf16[128,2176]{1,0:T(8,128)(2,1)S(1)}, bf16[128,2176]{1,0:T(8,128)(2,1)S(1)}, u32[]{:S(2)}, u32[]{:S(2)}) %collective-permute-start) | collective-permute-done | bytes 557088 | tf_op jit(solution)/shard_map/ppermute | solution.py:578
  24.3 1.6 collective-permute-start.9
  25.8 3.4 %collective-permute-start.6 = (bf16[128,2048]{1,0:T(8,128)(2,1)S(1)}, bf16[128,2048]{1,0:T(8,128)(2,1)S(1)}, u32[]{:S(2)}, u32[]{:S(2)}) collective-permute-start(bf16[128,2048]{1,0:T(8,128)(2,1)S(1)} %get-tuple-element.54), channel_id=1, source_target_pairs={{0,8},{4,12},{8,24},{12,28},{24,16},{28,20},{16,0},{20,4},{1,9},{5... | collective-permute-start | bytes 1572872 | tf_op jit(solution)/shard_map/ppermute | solution.py:578
  31.2 6.1 %collective-permute-done.1.refs_1_ = bf16[128,2176]{1,0:T(8,128)(2,1)S(1)} collective-permute-done((bf16[128,2176]{1,0:T(8,128)(2,1)S(1)}, bf16[128,2176]{1,0:T(8,128)(2,1)S(1)}, u32[]{:S(2)}, u32[]{:S(2)}) %collective-permute-start.1) | collective-permute-done | bytes 557088 | tf_op jit(solution)/shard_map/ppermute | solution.py:578
  39.2 8.6 %gate_up.2 = (bf16[2,704,256]{2,1,0:T(8,128)(2,1)S(1)}, f32[2,704,256]{2,1,0:T(8,128)S(1)}, f32[2,704,256]{2,1,0:T(8,128)S(1)}) custom-call(bf16[64,2048]{1,0:T(8,128)(2,1)S(1)} %get-tuple-element.51.refs_0_.refs_5_, bf16[64,2048]{1,0:T(8,128)(2,1)S(1)} %collective-permute-done.3.refs_5_.refs_1_.refs_6_, ...), custom_call_target="tpu_custom_call" | custom-call | flops 1024 | bytes 1024 | tf_op jit(solution)/shard_map/gate_up/pallas_call | solution.py:55
  49.7 2.8 %collective-permute-start.10 = (bf16[128,2048]{1,0:T(8,128)(2,1)S(1)}, bf16[128,2048]{1,0:T(8,128)(2,1)S(1)}, u32[]{:S(2)}, u32[]{:S(2)}) collective-permute-start(bf16[128,2048]{1,0:T(8,128)(2,1)S(1)} %get-tuple-element.61), channel_id=1, source_target_pairs={{0,8},{4,12},{8,24},{12,28},{24,16},{28,20},{16,0},{20,4},{1,9},{5... | collective-permute-start | bytes 1572872 | tf_op jit(solution)/shard_map/ppermute | solution.py:578
  56.1 13.9 %collective-permute-done.10.refs_4_ = bf16[128,2048]{1,0:T(8,128)(2,1)S(1)} collective-permute-done((bf16[128,2048]{1,0:T(8,128)(2,1)S(1)}, bf16[128,2048]{1,0:T(8,128)(2,1)S(1)}, u32[]{:S(2)}, u32[]{:S(2)}) %collective-permute-start.10) | collective-permute-done | bytes 524320 | tf_op jit(solution)/shard_map/ppermute | solution.py:578
  71.7 1.6 collective-permute-start.13
  75.3 12.5 %backward.2 = (bf16[8,64,2048]{2,1,0:T(8,128)(2,1)S(1)}, bf16[1408,256]{1,0:T(8,128)(2,1)}, bf16[1408,256]{1,0:T(8,128)(2,1)S(1)}) custom-call(s32[8]{0:T(128)S(1)} %stack.35.refs_0_, bf16[64,2048]{1,0:T(8,128)(2,1)S(1)} %get-tuple-element.68.refs_1_.refs_3_, bf16[2,64,2048]{2,1,0:T(8,128)(2,1)S(1)} %collective-permute-done.9.refs_3_.refs_2_.refs_4_.refs_8_, ...), custom_call_target="tpu_custom_call" | custom-call | flops 1024 | bytes 1024 | tf_op jit(solution)/shard_map/backward/pallas_call | solution.py:55
  87.8 1.6 collective-permute-start.19
  89.6 1.6 collective-permute-start.16
  91.2 8.9 %gate_up.3 = (bf16[2,704,256]{2,1,0:T(8,128)(2,1)S(1)}, f32[2,704,256]{2,1,0:T(8,128)S(1)}, f32[2,704,256]{2,1,0:T(8,128)S(1)}) custom-call(bf16[64,2048]{1,0:T(8,128)(2,1)S(1)} %get-tuple-element.62.refs_0_.refs_9_, bf16[2,64,2048]{2,1,0:T(8,128)(2,1)S(1)} %collective-permute-done.15.refs_4_.refs_1_.refs_6_.refs_10_, ...), custom_call_target="tpu_custom_call" | custom-call | flops 40000000000 | bytes 134217728 | tf_op jit(solution)/shard_map/gate_up/pallas_call | solution.py:55
  101.2 5.0 %grad_down.1 = (bf16[352,2048]{1,0:T(8,128)(2,1)}, bf16[352,2048]{1,0:T(8,128)(2,1)S(1)}, bf16[352,2048]{1,0:T(8,128)(2,1)}, bf16[352,2048]{1,0:T(8,128)(2,1)S(1)}) custom-call(s32[8]{0:T(128)S(1)} %stack.35.refs_0_, bf16[2,704,256]{2,1,0:T(8,128)(2,1)S(1)} %get-tuple-element.80.refs_1_, bf16[2,704,256]{2,1,0:T(8,128)(2,1)S(1)} %get-tuple-element.81.refs_2_, ...), custom_call_target="tpu_custom_call" | custom-call | flops 1024 | bytes 1024 | tf_op jit(solution)/shard_map/grad_down/pallas_call | solution.py:55
  108.0 12.7 %backward.3 = (bf16[8,64,2048]{2,1,0:T(8,128)(2,1)S(1)}, bf16[1408,256]{1,0:T(8,128)(2,1)}, bf16[1408,256]{1,0:T(8,128)(2,1)S(1)}) custom-call(s32[8]{0:T(128)S(1)} %stack.35.refs_0_, bf16[64,2048]{1,0:T(8,128)(2,1)S(1)} %get-tuple-element.64.refs_7_.refs_1_, ...), custom_call_target="tpu_custom_call", output_to_operand_aliasing={{0}: (8, {})} | custom-call | flops 40000000000 | bytes 134217728 | tf_op jit(solution)/shard_map/backward/pallas_call | solution.py:55
  123.5 4.7 %all-to-all-start = ((bf16[8,64,2048]{2,1,0:T(8,128)(2,1)}), bf16[8,64,2048]{2,1,0:T(8,128)(2,1)S(1)}, u32[]{:S(2)}, u32[]{:S(2)}) async-start(bf16[8,64,2048]{2,1,0:T(8,128)(2,1)} %copy-done.2), calls=%async_computation | async-start | bytes 4194304 | tf_op jit(solution)/shard_map/all_to_all | solution.py:647
  128.3 3.6 %add_convert_fusion.refs_21_ = bf16[352,2048]{1,0:T(8,128)(2,1)} fusion(bf16[352,2048]{1,0:T(8,128)(2,1)} %collective-permute-done.21, bf16[352,2048]{1,0:T(8,128)(2,1)} %copy-done.3), kind=kLoop, calls=%fused_computation | loop fusion | flops 2883584 | bytes 4325376 | tf_op jit(solution)/shard_map/convert_element_type | solution.py:649
  131.9 1.5 collective-permute-start.24
  133.5 8.8 %collective-permute-done.20.refs_4_ = bf16[1408,256]{1,0:T(8,128)(2,1)} collective-permute-done((bf16[1408,256]{1,0:T(8,128)(2,1)}, bf16[1408,256]{1,0:T(8,128)(2,1)}, u32[]{:S(2)}, u32[]{:S(2)}) %collective-permute-start.20) | collective-permute-done | bytes 720928 | tf_op jit(solution)/shard_map/ppermute | solution.py:587
  144.5 10.4 %grad_x.1 = (bf16[2,352,2048]{2,1,0:T(8,128)(2,1)}, bf16[2,352,2048]{2,1,0:T(8,128)(2,1)}) custom-call(s32[8]{0:T(128)S(1)} %stack.35.refs_0_, bf16[1408,256]{1,0:T(8,128)(2,1)S(1)} %copy-done.9, bf16[1408,256]{1,0:T(8,128)(2,1)S(1)} %copy-done.40, bf16[1408,256]{1,0:T(8,128)(2,1)} %collective-permute-done.19.refs_3_, ...), custom_call_target="tpu_custom_call" | custom-call | flops 40000000000 | bytes 134217728 | tf_op jit(solution)/shard_map/grad_x/pallas_call | solution.py:55
  155.0 21.3 %all-to-all-done = bf16[8,64,2048]{2,1,0:T(8,128)(2,1)S(1)} async-done(((bf16[8,64,2048]{2,1,0:T(8,128)(2,1)}), bf16[8,64,2048]{2,1,0:T(8,128)(2,1)S(1)}, u32[]{:S(2)}, u32[]{:S(2)}) %all-to-all-start) | async-done | bytes 2097184 | tf_op jit(solution)/shard_map/all_to_all | solution.py:647
  176.3 1.8 copy-done
  180.9 1.5 copy-done.1
  182.4 6.6 %sum_all.1 = bf16[352,6144]{1,0:T(8,128)(2,1)} custom-call(bf16[2,352,2048]{2,1,0:T(8,128)(2,1)S(1)} %copy-done.1, bf16[2,352,2048]{2,1,0:T(8,128)(2,1)} %collective-permute-done.23.refs_1_, bf16[352,2048]{1,0:T(8,128)(2,1)S(1)} %copy-done.5, bf16[352,2048]{1,0:T(8,128)(2,1)} %collective-permute-done.22.refs_22_.refs_3_, ...), custom_call_target="tpu_custom_call" | custom-call | flops 1024 | bytes 1024 | tf_op jit(solution)/shard_map/sum_all/pallas_call | solution.py:55
  (129 shorter events, 34.0 us)
Async XLA Ops:
  4.1 16.7 %collective-permute-start = (bf16[128,2176]{1,0:T(8,128)(2,1)S(1)}, bf16[128,2176]{1,0:T(8,128)(2,1)S(1)}, u32[]{:S(2)}, u32[]{:S(2)}) collective-permute-start(bf16[128,2176]{1,0:T(8,128)(2,1)S(1)} %get-tuple-element.48), channel_id=1, source_target_pairs={{0,8},{4,12},{8,24},{12,28},{24,16},{28,20},{16,0},{20,4},{1,9},{5... | collective-permute-start | bytes 1671176 | tf_op jit(solution)/shard_map/ppermute | solution.py:578
  7.2 14.6 %collective-permute-start.3 = (bf16[64,2048]{1,0:T(8,128)(2,1)S(1)}, bf16[64,2048]{1,0:T(8,128)(2,1)S(1)}, u32[]{:S(2)}, u32[]{:S(2)}) collective-permute-start(bf16[64,2048]{1,0:T(8,128)(2,1)S(1)} %get-tuple-element.50), channel_id=1, source_target_pairs={{0,4},{1,5},{2,6},{3,7},{4,0},{5,1},{6,2},{7,3},{8,12},{9,13},{10,... | collective-permute-start | bytes 786440 | tf_op jit(solution)/shard_map/ppermute | solution.py:587
  8.7 13.2 %collective-permute-start.4 = (bf16[64,2048]{1,0:T(8,128)(2,1)S(1)}, bf16[64,2048]{1,0:T(8,128)(2,1)S(1)}, u32[]{:S(2)}, u32[]{:S(2)}) collective-permute-start(bf16[64,2048]{1,0:T(8,128)(2,1)S(1)} %get-tuple-element.51.refs_0_.refs_5_), channel_id=1, source_target_pairs={{0,2},{1,3},{2,0},{3,1},{4,6},{5,7},{6,4},{7,5},{8,10},{9,11},{10,... | collective-permute-start | bytes 786440 | tf_op jit(solution)/shard_map/ppermute | solution.py:587
  20.9 16.5 %collective-permute-start.1 = (bf16[128,2176]{1,0:T(8,128)(2,1)S(1)}, bf16[128,2176]{1,0:T(8,128)(2,1)S(1)}, u32[]{:S(2)}, u32[]{:S(2)}) collective-permute-start(bf16[128,2176]{1,0:T(8,128)(2,1)S(1)} %collective-permute-done.refs_1_), channel_id=1, source_target_pairs={{0,8},{4,12},{8,24},{12,28},{24,16},{28,20},{16,0},{20,4},{1,9},{5... | collective-permute-start | bytes 1671176 | tf_op jit(solution)/shard_map/ppermute | solution.py:578
  24.3 14.9 %collective-permute-start.9 = (bf16[2,64,2048]{2,1,0:T(8,128)(2,1)S(1)}, bf16[2,64,2048]{2,1,0:T(8,128)(2,1)S(1)}, u32[]{:S(2)}, u32[]{:S(2)}) collective-permute-start(bf16[2,64,2048]{2,1,0:T(8,128)(2,1)S(1)} %get-tuple-element.57), channel_id=1, source_target_pairs={{0,4},{1,5},{2,6},{3,7},{4,0},{5,1},{6,2},{7,3},{8,12},{9,13},{10,... | collective-permute-start | bytes 1572872 | tf_op jit(solution)/shard_map/ppermute | solution.py:587
  25.8 22.7 %collective-permute-start.6 = (bf16[128,2048]{1,0:T(8,128)(2,1)S(1)}, bf16[128,2048]{1,0:T(8,128)(2,1)S(1)}, u32[]{:S(2)}, u32[]{:S(2)}) collective-permute-start(bf16[128,2048]{1,0:T(8,128)(2,1)S(1)} %get-tuple-element.54), channel_id=1, source_target_pairs={{0,8},{4,12},{8,24},{12,28},{24,16},{28,20},{16,0},{20,4},{1,9},{5... | collective-permute-start | bytes 1572872 | tf_op jit(solution)/shard_map/ppermute | solution.py:578
  29.2 18.7 %collective-permute-start.7 = (bf16[64,2048]{1,0:T(8,128)(2,1)S(1)}, bf16[64,2048]{1,0:T(8,128)(2,1)S(1)}, u32[]{:S(2)}, u32[]{:S(2)}) collective-permute-start(bf16[64,2048]{1,0:T(8,128)(2,1)S(1)} %get-tuple-element.55.refs_2_.refs_7_), channel_id=1, source_target_pairs={{0,2},{1,3},{2,0},{3,1},{4,6},{5,7},{6,4},{7,5},{8,10},{9,11},{10,... | collective-permute-start | bytes 786440 | tf_op jit(solution)/shard_map/ppermute | solution.py:587
  30.7 17.2 %collective-permute-start.8 = (bf16[64,2048]{1,0:T(8,128)(2,1)S(1)}, bf16[64,2048]{1,0:T(8,128)(2,1)S(1)}, u32[]{:S(2)}, u32[]{:S(2)}) collective-permute-start(bf16[64,2048]{1,0:T(8,128)(2,1)S(1)} %get-tuple-element.56), channel_id=1, source_target_pairs={{0,6},{1,7},{2,4},{3,5},{4,2},{5,3},{6,0},{7,1},{8,14},{9,15},{10,... | collective-permute-start | bytes 786440 | tf_op jit(solution)/shard_map/ppermute | solution.py:587
  37.3 33.2 %collective-permute-start.2 = (bf16[128,2176]{1,0:T(8,128)(2,1)S(1)}, bf16[128,2176]{1,0:T(8,128)(2,1)S(1)}, u32[]{:S(2)}, u32[]{:S(2)}) collective-permute-start(bf16[128,2176]{1,0:T(8,128)(2,1)S(1)} %collective-permute-done.1.refs_1_), channel_id=1, source_target_pairs={{0,8},{4,12},{8,24},{12,28},{24,16},{28,20},{16,0},{20,4},{1,9},{5... | collective-permute-start | bytes 1671176 | tf_op jit(solution)/shard_map/ppermute | solution.py:578
  49.7 20.2 %collective-permute-start.10 = (bf16[128,2048]{1,0:T(8,128)(2,1)S(1)}, bf16[128,2048]{1,0:T(8,128)(2,1)S(1)}, u32[]{:S(2)}, u32[]{:S(2)}) collective-permute-start(bf16[128,2048]{1,0:T(8,128)(2,1)S(1)} %get-tuple-element.61), channel_id=1, source_target_pairs={{0,8},{4,12},{8,24},{12,28},{24,16},{28,20},{16,0},{20,4},{1,9},{5... | collective-permute-start | bytes 1572872 | tf_op jit(solution)/shard_map/ppermute | solution.py:578
  52.6 17.9 %collective-permute-start.11 = (bf16[64,2048]{1,0:T(8,128)(2,1)S(1)}, bf16[64,2048]{1,0:T(8,128)(2,1)S(1)}, u32[]{:S(2)}, u32[]{:S(2)}) collective-permute-start(bf16[64,2048]{1,0:T(8,128)(2,1)S(1)} %get-tuple-element.62.refs_0_.refs_9_), channel_id=1, source_target_pairs={{0,2},{1,3},{2,0},{3,1},{4,6},{5,7},{6,4},{7,5},{8,10},{9,11},{10,... | collective-permute-start | bytes 786440 | tf_op jit(solution)/shard_map/ppermute | solution.py:587
  54.1 16.4 %collective-permute-start.12 = (bf16[64,2048]{1,0:T(8,128)(2,1)S(1)}, bf16[64,2048]{1,0:T(8,128)(2,1)S(1)}, u32[]{:S(2)}, u32[]{:S(2)}) collective-permute-start(bf16[64,2048]{1,0:T(8,128)(2,1)S(1)} %get-tuple-element.63), channel_id=1, source_target_pairs={{0,6},{1,7},{2,4},{3,5},{4,2},{5,3},{6,0},{7,1},{8,14},{9,15},{10,... | collective-permute-start | bytes 786440 | tf_op jit(solution)/shard_map/ppermute | solution.py:587
  55.5 19.7 %collective-permute-start.15 = (bf16[2,64,2048]{2,1,0:T(8,128)(2,1)S(1)}, bf16[2,64,2048]{2,1,0:T(8,128)(2,1)S(1)}, u32[]{:S(2)}, u32[]{:S(2)}) collective-permute-start(bf16[2,64,2048]{2,1,0:T(8,128)(2,1)S(1)} %get-tuple-element.70), channel_id=1, source_target_pairs={{0,4},{1,5},{2,6},{3,7},{4,0},{5,1},{6,2},{7,3},{8,12},{9,13},{10,... | collective-permute-start | bytes 1572872 | tf_op jit(solution)/shard_map/ppermute | solution.py:587
  70.0 19.4 %collective-permute-start.14 = (bf16[128,2048]{1,0:T(8,128)(2,1)S(1)}, bf16[128,2048]{1,0:T(8,128)(2,1)S(1)}, u32[]{:S(2)}, u32[]{:S(2)}) collective-permute-start(bf16[128,2048]{1,0:T(8,128)(2,1)S(1)} %collective-permute-done.10.refs_4_), channel_id=1, source_target_pairs={{0,8},{4,12},{8,24},{12,28},{24,16},{28,20},{16,0},{20,4},{1,9},{5... | collective-permute-start | bytes 1572872 | tf_op jit(solution)/shard_map/ppermute | solution.py:578
  71.7 19.5 %collective-permute-start.13 = (bf16[2,64,2048]{2,1,0:T(8,128)(2,1)S(1)}, bf16[2,64,2048]{2,1,0:T(8,128)(2,1)S(1)}, u32[]{:S(2)}, u32[]{:S(2)}) collective-permute-start(bf16[2,64,2048]{2,1,0:T(8,128)(2,1)S(1)} %get-tuple-element.65), channel_id=1, source_target_pairs={{0,4},{1,5},{2,6},{3,7},{4,0},{5,1},{6,2},{7,3},{8,12},{9,13},{10,... | collective-permute-start | bytes 1572872 | tf_op jit(solution)/shard_map/ppermute | solution.py:587
  73.2 34.7 %collective-permute-start.17 = (bf16[64,2048]{1,0:T(8,128)(2,1)S(1)}, bf16[64,2048]{1,0:T(8,128)(2,1)S(1)}, u32[]{:S(2)}, u32[]{:S(2)}) collective-permute-start(bf16[64,2048]{1,0:T(8,128)(2,1)S(1)} %get-tuple-element.75.refs_2_.refs_11_), channel_id=1, source_target_pairs={{0,2},{1,3},{2,0},{3,1},{4,6},{5,7},{6,4},{7,5},{8,10},{9,11},{10,... | collective-permute-start | bytes 786440 | tf_op jit(solution)/shard_map/ppermute | solution.py:587
  74.8 33.2 %collective-permute-start.18 = (bf16[64,2048]{1,0:T(8,128)(2,1)S(1)}, bf16[64,2048]{1,0:T(8,128)(2,1)S(1)}, u32[]{:S(2)}, u32[]{:S(2)}) collective-permute-start(bf16[64,2048]{1,0:T(8,128)(2,1)S(1)} %get-tuple-element.79), channel_id=1, source_target_pairs={{0,6},{1,7},{2,4},{3,5},{4,2},{5,3},{6,0},{7,1},{8,14},{9,15},{10,... | collective-permute-start | bytes 786440 | tf_op jit(solution)/shard_map/ppermute | solution.py:587
  87.8 45.7 %collective-permute-start.19 = (bf16[1408,256]{1,0:T(8,128)(2,1)}, bf16[1408,256]{1,0:T(8,128)(2,1)}, u32[]{:S(2)}, u32[]{:S(2)}) collective-permute-start(bf16[1408,256]{1,0:T(8,128)(2,1)} %get-tuple-element.85), channel_id=1, source_target_pairs={{0,2},{1,3},{2,0},{3,1},{4,6},{5,7},{6,4},{7,5},{8,10},{9,11},{10,... | collective-permute-start | bytes 2162696 | tf_op jit(solution)/shard_map/ppermute | solution.py:587
  107.4 20.7 %collective-permute-start.21 = (bf16[352,2048]{1,0:T(8,128)(2,1)}, bf16[352,2048]{1,0:T(8,128)(2,1)}, u32[]{:S(2)}, u32[]{:S(2)}) collective-permute-start(bf16[352,2048]{1,0:T(8,128)(2,1)} %get-tuple-element.88), channel_id=1, source_target_pairs={{0,1},{1,0},{2,3},{3,2},{4,5},{5,4},{6,7},{7,6},{8,9},{9,8},{10,11... | collective-permute-start | bytes 4325384 | tf_op jit(solution)/shard_map/ppermute | solution.py:587
  107.4 34.9 %collective-permute-start.22 = (bf16[352,2048]{1,0:T(8,128)(2,1)}, bf16[352,2048]{1,0:T(8,128)(2,1)}, u32[]{:S(2)}, u32[]{:S(2)}) collective-permute-start(bf16[352,2048]{1,0:T(8,128)(2,1)} %get-tuple-element.89), channel_id=1, source_target_pairs={{0,1},{1,0},{2,3},{3,2},{4,5},{5,4},{6,7},{7,6},{8,9},{9,8},{10,11... | collective-permute-start | bytes 4325384 | tf_op jit(solution)/shard_map/ppermute | solution.py:587
  123.0 19.3 %collective-permute-start.20 = (bf16[1408,256]{1,0:T(8,128)(2,1)}, bf16[1408,256]{1,0:T(8,128)(2,1)}, u32[]{:S(2)}, u32[]{:S(2)}) collective-permute-start(bf16[1408,256]{1,0:T(8,128)(2,1)} %get-tuple-element.86), channel_id=1, source_target_pairs={{0,2},{1,3},{2,0},{3,1},{4,6},{5,7},{6,4},{7,5},{8,10},{9,11},{10,... | collective-permute-start | bytes 2162696 | tf_op jit(solution)/shard_map/ppermute | solution.py:587
  123.5 52.8 %all-to-all-start = ((bf16[8,64,2048]{2,1,0:T(8,128)(2,1)}), bf16[8,64,2048]{2,1,0:T(8,128)(2,1)S(1)}, u32[]{:S(2)}, u32[]{:S(2)}) async-start(bf16[8,64,2048]{2,1,0:T(8,128)(2,1)} %copy-done.2), calls=%async_computation | async-start | bytes 4194304 | tf_op jit(solution)/shard_map/all_to_all | solution.py:647
  131.9 47.4 %collective-permute-start.24 = (bf16[352,2048]{1,0:T(8,128)(2,1)}, bf16[352,2048]{1,0:T(8,128)(2,1)}, u32[]{:S(2)}, u32[]{:S(2)}) collective-permute-start(bf16[352,2048]{1,0:T(8,128)(2,1)} %add_convert_fusion.refs_21_), channel_id=1, source_target_pairs={{0,2},{1,3},{2,0},{3,1},{4,6},{5,7},{6,4},{7,5},{8,10},{9,11},{10,... | collective-permute-start | bytes 4325384 | tf_op jit(solution)/shard_map/ppermute | solution.py:587
  154.9 25.6 %collective-permute-start.23 = (bf16[2,352,2048]{2,1,0:T(8,128)(2,1)}, bf16[2,352,2048]{2,1,0:T(8,128)(2,1)}, u32[]{:S(2)}, u32[]{:S(2)}) collective-permute-start(bf16[2,352,2048]{2,1,0:T(8,128)(2,1)} %get-tuple-element.91), channel_id=1, source_target_pairs={{0,1},{1,0},{2,3},{3,2},{4,5},{5,4},{6,7},{7,6},{8,9},{9,8},{10,11... | collective-permute-start | bytes 8650760 | tf_op jit(solution)/shard_map/ppermute | solution.py:587
  (43 other events, 481.6 us)

commit v4 on v2

--- a/solution.py
+++ b/solution.py
@@ -426,7 +426,7 @@
     left = jnp.concatenate(lefts, axis=0)
     for copy in copies:
         copy.wait()
-    tile = tile_of(width, 512)
+    tile = tile_of(width, 1024)
     for n in range(0, width, tile):
         columns = slice(n, n + tile)
         total = jnp.dot(left, right[:, columns], preferred_element_type=F32).astype(BF16)
@@ -466,7 +466,7 @@
                 jnp.concatenate([ref[lead, pl.ds(start, own), :] for ref in hids], axis=1)
             )
     left = jnp.concatenate(lefts, axis=0)
-    tile = tile_of(width, 512)
+    tile = tile_of(width, 1024)
     for n in range(0, width, tile):
         columns = slice(n, n + tile)
         right = side_by_side(rows, whiches, columns)

time: 184 us -> 184 us (level)
  no operation moved by 1% of the time
where the time goes in v4:
time: 184 us; the launch traced here: 183 us
  Pallas kernels  67.5 us (37%)
  waiting for transfers between devices  58.8 us (32%)
  starting transfers between devices  36 us (20%)
  local copies, waits for them, and re-layouts  15.1 us (8%)
  other arithmetic  3.95 us (2%)
    pallas_call x15, Pallas kernels, call(): pl.pallas_call(body_of, in_specs=list(specs) + [anywhere()] * len(extra),...  67.5 us
    ppermute x6, waiting for transfers between devices, along_ring(): return lax.ppermute(value, 'expert', pairs)  30.7 us
    ppermute x19, waiting for transfers between devices, across(): return lax.ppermute(value, ('expert', 'replica'), pairs)  28.1 us
    ppermute x19, starting transfers between devices, across(): return lax.ppermute(value, ('expert', 'replica'), pairs)  19.9 us
    unnamed x86, local copies, waits for them, and re-layouts  15 us
    ppermute x6, starting transfers between devices, along_ring(): return lax.ppermute(value, 'expert', pairs)  11.5 us
    all_to_all x1, starting transfers between devices, body(): lax.all_to_all(dx, 'expert', split_axis=0, concat_axis=0, tiled=True)  4.66 us
  transfers between devices with their start and end apart: 26, of which 7 were waited for; matrix products, arithmetic and copies ran while one was open for 1% of the time, Pallas kernels for 36%

profile of v4, /device:TPU:0, one launch (start us, length us, event | category | flops | bytes accessed | tf_op | source)
XLA Modules:
  0.0 182.8 jit_solution(3849537547868595254)
XLA Ops:
  4.1 3.1 %collective-permute-start = (bf16[128,2176]{1,0:T(8,128)(2,1)S(1)}, bf16[128,2176]{1,0:T(8,128)(2,1)S(1)}, u32[]{:S(2)}, u32[]{:S(2)}) collective-permute-start(bf16[128,2176]{1,0:T(8,128)(2,1)S(1)} %get-tuple-element.48), channel_id=1, source_target_pairs={{0,8},{4,12},{8,24},{12,28},{24,16},{28,20},{16,0},{20,4},{1,9},{5... | collective-permute-start | bytes 1671176 | tf_op jit(solution)/shard_map/ppermute | solution.py:578
  10.7 10.2 %collective-permute-done.refs_1_ = bf16[128,2176]{1,0:T(8,128)(2,1)S(1)} collective-permute-done((bf16[128,2176]{1,0:T(8,128)(2,1)S(1)}, bf16[128,2176]{1,0:T(8,128)(2,1)S(1)}, u32[]{:S(2)}, u32[]{:S(2)}) %collective-permute-start) | collective-permute-done | bytes 557088 | tf_op jit(solution)/shard_map/ppermute | solution.py:578
  24.3 1.6 collective-permute-start.9
  25.9 3.4 %collective-permute-start.6 = (bf16[128,2048]{1,0:T(8,128)(2,1)S(1)}, bf16[128,2048]{1,0:T(8,128)(2,1)S(1)}, u32[]{:S(2)}, u32[]{:S(2)}) collective-permute-start(bf16[128,2048]{1,0:T(8,128)(2,1)S(1)} %get-tuple-element.54), channel_id=1, source_target_pairs={{0,8},{4,12},{8,24},{12,28},{24,16},{28,20},{16,0},{20,4},{1,9},{5... | collective-permute-start | bytes 1572872 | tf_op jit(solution)/shard_map/ppermute | solution.py:578
  31.2 6.1 %collective-permute-done.1.refs_1_ = bf16[128,2176]{1,0:T(8,128)(2,1)S(1)} collective-permute-done((bf16[128,2176]{1,0:T(8,128)(2,1)S(1)}, bf16[128,2176]{1,0:T(8,128)(2,1)S(1)}, u32[]{:S(2)}, u32[]{:S(2)}) %collective-permute-start.1) | collective-permute-done | bytes 557088 | tf_op jit(solution)/shard_map/ppermute | solution.py:578
  39.2 8.6 %gate_up.2 = (bf16[2,704,256]{2,1,0:T(8,128)(2,1)S(1)}, f32[2,704,256]{2,1,0:T(8,128)S(1)}, f32[2,704,256]{2,1,0:T(8,128)S(1)}) custom-call(bf16[64,2048]{1,0:T(8,128)(2,1)S(1)} %get-tuple-element.51.refs_0_.refs_5_, bf16[64,2048]{1,0:T(8,128)(2,1)S(1)} %collective-permute-done.3.refs_5_.refs_1_.refs_6_, ...), custom_call_target="tpu_custom_call" | custom-call | flops 1024 | bytes 1024 | tf_op jit(solution)/shard_map/gate_up/pallas_call | solution.py:55
  49.7 2.9 %collective-permute-start.10 = (bf16[128,2048]{1,0:T(8,128)(2,1)S(1)}, bf16[128,2048]{1,0:T(8,128)(2,1)S(1)}, u32[]{:S(2)}, u32[]{:S(2)}) collective-permute-start(bf16[128,2048]{1,0:T(8,128)(2,1)S(1)} %get-tuple-element.61), channel_id=1, source_target_pairs={{0,8},{4,12},{8,24},{12,28},{24,16},{28,20},{16,0},{20,4},{1,9},{5... | collective-permute-start | bytes 1572872 | tf_op jit(solution)/shard_map/ppermute | solution.py:578
  56.1 13.9 %collective-permute-done.10.refs_4_ = bf16[128,2048]{1,0:T(8,128)(2,1)S(1)} collective-permute-done((bf16[128,2048]{1,0:T(8,128)(2,1)S(1)}, bf16[128,2048]{1,0:T(8,128)(2,1)S(1)}, u32[]{:S(2)}, u32[]{:S(2)}) %collective-permute-start.10) | collective-permute-done | bytes 524320 | tf_op jit(solution)/shard_map/ppermute | solution.py:578
  71.7 1.6 collective-permute-start.13
  75.3 12.5 %backward.2 = (bf16[8,64,2048]{2,1,0:T(8,128)(2,1)S(1)}, bf16[1408,256]{1,0:T(8,128)(2,1)}, bf16[1408,256]{1,0:T(8,128)(2,1)S(1)}) custom-call(s32[8]{0:T(128)S(1)} %stack.35.refs_0_, bf16[64,2048]{1,0:T(8,128)(2,1)S(1)} %get-tuple-element.68.refs_1_.refs_3_, bf16[2,64,2048]{2,1,0:T(8,128)(2,1)S(1)} %collective-permute-done.9.refs_3_.refs_2_.refs_4_.refs_8_, ...), custom_call_target="tpu_custom_call" | custom-call | flops 1024 | bytes 1024 | tf_op jit(solution)/shard_map/backward/pallas_call | solution.py:55
  87.7 1.6 collective-permute-start.19
  91.2 8.9 %gate_up.3 = (bf16[2,704,256]{2,1,0:T(8,128)(2,1)S(1)}, f32[2,704,256]{2,1,0:T(8,128)S(1)}, f32[2,704,256]{2,1,0:T(8,128)S(1)}) custom-call(bf16[64,2048]{1,0:T(8,128)(2,1)S(1)} %get-tuple-element.62.refs_0_.refs_9_, bf16[2,64,2048]{2,1,0:T(8,128)(2,1)S(1)} %collective-permute-done.15.refs_4_.refs_1_.refs_6_.refs_10_, ...), custom_call_target="tpu_custom_call" | custom-call | flops 40000000000 | bytes 134217728 | tf_op jit(solution)/shard_map/gate_up/pallas_call | solution.py:55
  101.2 5.0 %grad_down.1 = (bf16[352,2048]{1,0:T(8,128)(2,1)}, bf16[352,2048]{1,0:T(8,128)(2,1)S(1)}, bf16[352,2048]{1,0:T(8,128)(2,1)}, bf16[352,2048]{1,0:T(8,128)(2,1)S(1)}) custom-call(s32[8]{0:T(128)S(1)} %stack.35.refs_0_, bf16[2,704,256]{2,1,0:T(8,128)(2,1)S(1)} %get-tuple-element.80.refs_1_, bf16[2,704,256]{2,1,0:T(8,128)(2,1)S(1)} %get-tuple-element.81.refs_2_, ...), custom_call_target="tpu_custom_call" | custom-call | flops 1024 | bytes 1024 | tf_op jit(solution)/shard_map/grad_down/pallas_call | solution.py:55
  107.9 12.7 %backward.3 = (bf16[8,64,2048]{2,1,0:T(8,128)(2,1)S(1)}, bf16[1408,256]{1,0:T(8,128)(2,1)}, bf16[1408,256]{1,0:T(8,128)(2,1)S(1)}) custom-call(s32[8]{0:T(128)S(1)} %stack.35.refs_0_, bf16[64,2048]{1,0:T(8,128)(2,1)S(1)} %get-tuple-element.64.refs_7_.refs_1_, ...), custom_call_target="tpu_custom_call", output_to_operand_aliasing={{0}: (8, {})} | custom-call | flops 40000000000 | bytes 134217728 | tf_op jit(solution)/shard_map/backward/pallas_call | solution.py:55
  123.3 4.7 %all-to-all-start = ((bf16[8,64,2048]{2,1,0:T(8,128)(2,1)}), bf16[8,64,2048]{2,1,0:T(8,128)(2,1)S(1)}, u32[]{:S(2)}, u32[]{:S(2)}) async-start(bf16[8,64,2048]{2,1,0:T(8,128)(2,1)} %copy-done.3), calls=%async_computation | async-start | bytes 4194304 | tf_op jit(solution)/shard_map/all_to_all | solution.py:647
  128.1 2.6 %add_convert_fusion.refs_21_ = bf16[352,2048]{1,0:T(8,128)(2,1)S(1)} fusion(bf16[352,2048]{1,0:T(8,128)(2,1)} %collective-permute-done.21, bf16[352,2048]{1,0:T(8,128)(2,1)} %copy-done.4), kind=kLoop, calls=%fused_computation | loop fusion | flops 2883584 | bytes 4325376 | tf_op jit(solution)/shard_map/convert_element_type | solution.py:649
  130.7 1.6 collective-permute-start.24
  132.3 9.8 %collective-permute-done.20.refs_4_ = bf16[1408,256]{1,0:T(8,128)(2,1)} collective-permute-done((bf16[1408,256]{1,0:T(8,128)(2,1)}, bf16[1408,256]{1,0:T(8,128)(2,1)}, u32[]{:S(2)}, u32[]{:S(2)}) %collective-permute-start.20) | collective-permute-done | bytes 720928 | tf_op jit(solution)/shard_map/ppermute | solution.py:587
  144.3 10.4 %grad_x.1 = (bf16[2,352,2048]{2,1,0:T(8,128)(2,1)}, bf16[2,352,2048]{2,1,0:T(8,128)(2,1)}) custom-call(s32[8]{0:T(128)S(1)} %stack.35.refs_0_, bf16[1408,256]{1,0:T(8,128)(2,1)S(1)} %copy-done.12, bf16[1408,256]{1,0:T(8,128)(2,1)S(1)} %copy-done.42, bf16[1408,256]{1,0:T(8,128)(2,1)} %collective-permute-done.19.refs_3_, ...), custom_call_target="tpu_custom_call" | custom-call | flops 40000000000 | bytes 134217728 | tf_op jit(solution)/shard_map/grad_x/pallas_call | solution.py:55
  154.8 17.1 %collective-permute-done.24.refs_0_.refs_4_ = bf16[352,2048]{1,0:T(8,128)(2,1)S(1)} collective-permute-done((bf16[352,2048]{1,0:T(8,128)(2,1)S(1)}, bf16[352,2048]{1,0:T(8,128)(2,1)S(1)}, u32[]{:S(2)}, u32[]{:S(2)}) %collective-permute-start.24) | collective-permute-done | bytes 1441824 | tf_op jit(solution)/shard_map/ppermute | solution.py:587
  172.0 1.8 copy-done.1
  173.8 1.8 copy-done.2
  176.0 3.3 %sum_all.1.refs_2_ = bf16[352,6144]{1,0:T(8,128)(2,1)} custom-call(bf16[2,352,2048]{2,1,0:T(8,128)(2,1)S(1)} %copy-done.2, bf16[2,352,2048]{2,1,0:T(8,128)(2,1)S(1)} %collective-permute-done.23.refs_1_, bf16[352,2048]{1,0:T(8,128)(2,1)S(1)} %copy-done.6, bf16[352,2048]{1,0:T(8,128)(2,1)} %collective-permute-done.22.refs_22_.refs_3_, ...), custom_call_target="tpu_custom_call" | custom-call | flops 1024 | bytes 1024 | tf_op jit(solution)/shard_map/sum_all/pallas_call | solution.py:55
  179.3 2.2 %copy-done = bf16[352,6144]{1,0:T(8,128)(2,1)S(1)} copy-done((bf16[352,6144]{1,0:T(8,128)(2,1)S(1)}, bf16[352,6144]{1,0:T(8,128)(2,1)}, u32[]{:S(2)}) %copy-start) | copy-done | bytes 4325400
  (133 shorter events, 34.3 us)
Async XLA Ops:
  4.1 16.7 %collective-permute-start = (bf16[128,2176]{1,0:T(8,128)(2,1)S(1)}, bf16[128,2176]{1,0:T(8,128)(2,1)S(1)}, u32[]{:S(2)}, u32[]{:S(2)}) collective-permute-start(bf16[128,2176]{1,0:T(8,128)(2,1)S(1)} %get-tuple-element.48), channel_id=1, source_target_pairs={{0,8},{4,12},{8,24},{12,28},{24,16},{28,20},{16,0},{20,4},{1,9},{5... | collective-permute-start | bytes 1671176 | tf_op jit(solution)/shard_map/ppermute | solution.py:578
  7.2 14.7 %collective-permute-start.3 = (bf16[64,2048]{1,0:T(8,128)(2,1)S(1)}, bf16[64,2048]{1,0:T(8,128)(2,1)S(1)}, u32[]{:S(2)}, u32[]{:S(2)}) collective-permute-start(bf16[64,2048]{1,0:T(8,128)(2,1)S(1)} %get-tuple-element.50), channel_id=1, source_target_pairs={{0,4},{1,5},{2,6},{3,7},{4,0},{5,1},{6,2},{7,3},{8,12},{9,13},{10,... | collective-permute-start | bytes 786440 | tf_op jit(solution)/shard_map/ppermute | solution.py:587
  8.7 13.2 %collective-permute-start.4 = (bf16[64,2048]{1,0:T(8,128)(2,1)S(1)}, bf16[64,2048]{1,0:T(8,128)(2,1)S(1)}, u32[]{:S(2)}, u32[]{:S(2)}) collective-permute-start(bf16[64,2048]{1,0:T(8,128)(2,1)S(1)} %get-tuple-element.51.refs_0_.refs_5_), channel_id=1, source_target_pairs={{0,2},{1,3},{2,0},{3,1},{4,6},{5,7},{6,4},{7,5},{8,10},{9,11},{10,... | collective-permute-start | bytes 786440 | tf_op jit(solution)/shard_map/ppermute | solution.py:587
  20.9 16.5 %collective-permute-start.1 = (bf16[128,2176]{1,0:T(8,128)(2,1)S(1)}, bf16[128,2176]{1,0:T(8,128)(2,1)S(1)}, u32[]{:S(2)}, u32[]{:S(2)}) collective-permute-start(bf16[128,2176]{1,0:T(8,128)(2,1)S(1)} %collective-permute-done.refs_1_), channel_id=1, source_target_pairs={{0,8},{4,12},{8,24},{12,28},{24,16},{28,20},{16,0},{20,4},{1,9},{5... | collective-permute-start | bytes 1671176 | tf_op jit(solution)/shard_map/ppermute | solution.py:578
  24.3 14.9 %collective-permute-start.9 = (bf16[2,64,2048]{2,1,0:T(8,128)(2,1)S(1)}, bf16[2,64,2048]{2,1,0:T(8,128)(2,1)S(1)}, u32[]{:S(2)}, u32[]{:S(2)}) collective-permute-start(bf16[2,64,2048]{2,1,0:T(8,128)(2,1)S(1)} %get-tuple-element.57), channel_id=1, source_target_pairs={{0,4},{1,5},{2,6},{3,7},{4,0},{5,1},{6,2},{7,3},{8,12},{9,13},{10,... | collective-permute-start | bytes 1572872 | tf_op jit(solution)/shard_map/ppermute | solution.py:587
  25.9 22.7 %collective-permute-start.6 = (bf16[128,2048]{1,0:T(8,128)(2,1)S(1)}, bf16[128,2048]{1,0:T(8,128)(2,1)S(1)}, u32[]{:S(2)}, u32[]{:S(2)}) collective-permute-start(bf16[128,2048]{1,0:T(8,128)(2,1)S(1)} %get-tuple-element.54), channel_id=1, source_target_pairs={{0,8},{4,12},{8,24},{12,28},{24,16},{28,20},{16,0},{20,4},{1,9},{5... | collective-permute-start | bytes 1572872 | tf_op jit(solution)/shard_map/ppermute | solution.py:578
  29.2 18.7 %collective-permute-start.7 = (bf16[64,2048]{1,0:T(8,128)(2,1)S(1)}, bf16[64,2048]{1,0:T(8,128)(2,1)S(1)}, u32[]{:S(2)}, u32[]{:S(2)}) collective-permute-start(bf16[64,2048]{1,0:T(8,128)(2,1)S(1)} %get-tuple-element.55.refs_2_.refs_7_), channel_id=1, source_target_pairs={{0,2},{1,3},{2,0},{3,1},{4,6},{5,7},{6,4},{7,5},{8,10},{9,11},{10,... | collective-permute-start | bytes 786440 | tf_op jit(solution)/shard_map/ppermute | solution.py:587
  30.8 17.2 %collective-permute-start.8 = (bf16[64,2048]{1,0:T(8,128)(2,1)S(1)}, bf16[64,2048]{1,0:T(8,128)(2,1)S(1)}, u32[]{:S(2)}, u32[]{:S(2)}) collective-permute-start(bf16[64,2048]{1,0:T(8,128)(2,1)S(1)} %get-tuple-element.56), channel_id=1, source_target_pairs={{0,6},{1,7},{2,4},{3,5},{4,2},{5,3},{6,0},{7,1},{8,14},{9,15},{10,... | collective-permute-start | bytes 786440 | tf_op jit(solution)/shard_map/ppermute | solution.py:587
  37.3 33.2 %collective-permute-start.2 = (bf16[128,2176]{1,0:T(8,128)(2,1)S(1)}, bf16[128,2176]{1,0:T(8,128)(2,1)S(1)}, u32[]{:S(2)}, u32[]{:S(2)}) collective-permute-start(bf16[128,2176]{1,0:T(8,128)(2,1)S(1)} %collective-permute-done.1.refs_1_), channel_id=1, source_target_pairs={{0,8},{4,12},{8,24},{12,28},{24,16},{28,20},{16,0},{20,4},{1,9},{5... | collective-permute-start | bytes 1671176 | tf_op jit(solution)/shard_map/ppermute | solution.py:578
  49.7 20.2 %collective-permute-start.10 = (bf16[128,2048]{1,0:T(8,128)(2,1)S(1)}, bf16[128,2048]{1,0:T(8,128)(2,1)S(1)}, u32[]{:S(2)}, u32[]{:S(2)}) collective-permute-start(bf16[128,2048]{1,0:T(8,128)(2,1)S(1)} %get-tuple-element.61), channel_id=1, source_target_pairs={{0,8},{4,12},{8,24},{12,28},{24,16},{28,20},{16,0},{20,4},{1,9},{5... | collective-permute-start | bytes 1572872 | tf_op jit(solution)/shard_map/ppermute | solution.py:578
  52.6 17.9 %collective-permute-start.11 = (bf16[64,2048]{1,0:T(8,128)(2,1)S(1)}, bf16[64,2048]{1,0:T(8,128)(2,1)S(1)}, u32[]{:S(2)}, u32[]{:S(2)}) collective-permute-start(bf16[64,2048]{1,0:T(8,128)(2,1)S(1)} %get-tuple-element.62.refs_0_.refs_9_), channel_id=1, source_target_pairs={{0,2},{1,3},{2,0},{3,1},{4,6},{5,7},{6,4},{7,5},{8,10},{9,11},{10,... | collective-permute-start | bytes 786440 | tf_op jit(solution)/shard_map/ppermute | solution.py:587
  54.1 16.4 %collective-permute-start.12 = (bf16[64,2048]{1,0:T(8,128)(2,1)S(1)}, bf16[64,2048]{1,0:T(8,128)(2,1)S(1)}, u32[]{:S(2)}, u32[]{:S(2)}) collective-permute-start(bf16[64,2048]{1,0:T(8,128)(2,1)S(1)} %get-tuple-element.63), channel_id=1, source_target_pairs={{0,6},{1,7},{2,4},{3,5},{4,2},{5,3},{6,0},{7,1},{8,14},{9,15},{10,... | collective-permute-start | bytes 786440 | tf_op jit(solution)/shard_map/ppermute | solution.py:587
  55.5 19.7 %collective-permute-start.15 = (bf16[2,64,2048]{2,1,0:T(8,128)(2,1)S(1)}, bf16[2,64,2048]{2,1,0:T(8,128)(2,1)S(1)}, u32[]{:S(2)}, u32[]{:S(2)}) collective-permute-start(bf16[2,64,2048]{2,1,0:T(8,128)(2,1)S(1)} %get-tuple-element.70), channel_id=1, source_target_pairs={{0,4},{1,5},{2,6},{3,7},{4,0},{5,1},{6,2},{7,3},{8,12},{9,13},{10,... | collective-permute-start | bytes 1572872 | tf_op jit(solution)/shard_map/ppermute | solution.py:587
  70.0 19.4 %collective-permute-start.14 = (bf16[128,2048]{1,0:T(8,128)(2,1)S(1)}, bf16[128,2048]{1,0:T(8,128)(2,1)S(1)}, u32[]{:S(2)}, u32[]{:S(2)}) collective-permute-start(bf16[128,2048]{1,0:T(8,128)(2,1)S(1)} %collective-permute-done.10.refs_4_), channel_id=1, source_target_pairs={{0,8},{4,12},{8,24},{12,28},{24,16},{28,20},{16,0},{20,4},{1,9},{5... | collective-permute-start | bytes 1572872 | tf_op jit(solution)/shard_map/ppermute | solution.py:578
  71.7 19.5 %collective-permute-start.13 = (bf16[2,64,2048]{2,1,0:T(8,128)(2,1)S(1)}, bf16[2,64,2048]{2,1,0:T(8,128)(2,1)S(1)}, u32[]{:S(2)}, u32[]{:S(2)}) collective-permute-start(bf16[2,64,2048]{2,1,0:T(8,128)(2,1)S(1)} %get-tuple-element.65), channel_id=1, source_target_pairs={{0,4},{1,5},{2,6},{3,7},{4,0},{5,1},{6,2},{7,3},{8,12},{9,13},{10,... | collective-permute-start | bytes 1572872 | tf_op jit(solution)/shard_map/ppermute | solution.py:587
  73.2 34.6 %collective-permute-start.17 = (bf16[64,2048]{1,0:T(8,128)(2,1)S(1)}, bf16[64,2048]{1,0:T(8,128)(2,1)S(1)}, u32[]{:S(2)}, u32[]{:S(2)}) collective-permute-start(bf16[64,2048]{1,0:T(8,128)(2,1)S(1)} %get-tuple-element.75.refs_2_.refs_11_), channel_id=1, source_target_pairs={{0,2},{1,3},{2,0},{3,1},{4,6},{5,7},{6,4},{7,5},{8,10},{9,11},{10,... | collective-permute-start | bytes 786440 | tf_op jit(solution)/shard_map/ppermute | solution.py:587
  74.8 33.1 %collective-permute-start.18 = (bf16[64,2048]{1,0:T(8,128)(2,1)S(1)}, bf16[64,2048]{1,0:T(8,128)(2,1)S(1)}, u32[]{:S(2)}, u32[]{:S(2)}) collective-permute-start(bf16[64,2048]{1,0:T(8,128)(2,1)S(1)} %get-tuple-element.79), channel_id=1, source_target_pairs={{0,6},{1,7},{2,4},{3,5},{4,2},{5,3},{6,0},{7,1},{8,14},{9,15},{10,... | collective-permute-start | bytes 786440 | tf_op jit(solution)/shard_map/ppermute | solution.py:587
  87.7 44.5 %collective-permute-start.19 = (bf16[1408,256]{1,0:T(8,128)(2,1)}, bf16[1408,256]{1,0:T(8,128)(2,1)}, u32[]{:S(2)}, u32[]{:S(2)}) collective-permute-start(bf16[1408,256]{1,0:T(8,128)(2,1)} %get-tuple-element.85), channel_id=1, source_target_pairs={{0,2},{1,3},{2,0},{3,1},{4,6},{5,7},{6,4},{7,5},{8,10},{9,11},{10,... | collective-permute-start | bytes 2162696 | tf_op jit(solution)/shard_map/ppermute | solution.py:587
  107.3 20.6 %collective-permute-start.21 = (bf16[352,2048]{1,0:T(8,128)(2,1)}, bf16[352,2048]{1,0:T(8,128)(2,1)}, u32[]{:S(2)}, u32[]{:S(2)}) collective-permute-start(bf16[352,2048]{1,0:T(8,128)(2,1)} %get-tuple-element.88), channel_id=1, source_target_pairs={{0,1},{1,0},{2,3},{3,2},{4,5},{5,4},{6,7},{7,6},{8,9},{9,8},{10,11... | collective-permute-start | bytes 4325384 | tf_op jit(solution)/shard_map/ppermute | solution.py:587
  107.3 34.8 %collective-permute-start.22 = (bf16[352,2048]{1,0:T(8,128)(2,1)}, bf16[352,2048]{1,0:T(8,128)(2,1)}, u32[]{:S(2)}, u32[]{:S(2)}) collective-permute-start(bf16[352,2048]{1,0:T(8,128)(2,1)} %get-tuple-element.89), channel_id=1, source_target_pairs={{0,1},{1,0},{2,3},{3,2},{4,5},{5,4},{6,7},{7,6},{8,9},{9,8},{10,11... | collective-permute-start | bytes 4325384 | tf_op jit(solution)/shard_map/ppermute | solution.py:587
  122.8 19.3 %collective-permute-start.20 = (bf16[1408,256]{1,0:T(8,128)(2,1)}, bf16[1408,256]{1,0:T(8,128)(2,1)}, u32[]{:S(2)}, u32[]{:S(2)}) collective-permute-start(bf16[1408,256]{1,0:T(8,128)(2,1)} %get-tuple-element.86), channel_id=1, source_target_pairs={{0,2},{1,3},{2,0},{3,1},{4,6},{5,7},{6,4},{7,5},{8,10},{9,11},{10,... | collective-permute-start | bytes 2162696 | tf_op jit(solution)/shard_map/ppermute | solution.py:587
  123.3 56.0 %all-to-all-start = ((bf16[8,64,2048]{2,1,0:T(8,128)(2,1)}), bf16[8,64,2048]{2,1,0:T(8,128)(2,1)S(1)}, u32[]{:S(2)}, u32[]{:S(2)}) async-start(bf16[8,64,2048]{2,1,0:T(8,128)(2,1)} %copy-done.3), calls=%async_computation | async-start | bytes 4194304 | tf_op jit(solution)/shard_map/all_to_all | solution.py:647
  130.7 41.3 %collective-permute-start.24 = (bf16[352,2048]{1,0:T(8,128)(2,1)S(1)}, bf16[352,2048]{1,0:T(8,128)(2,1)S(1)}, u32[]{:S(2)}, u32[]{:S(2)}) collective-permute-start(bf16[352,2048]{1,0:T(8,128)(2,1)S(1)} %add_convert_fusion.refs_21_), channel_id=1, source_target_pairs={{0,2},{1,3},{2,0},{3,1},{4,6},{5,7},{6,4},{7,5},{8,10},{9,11},{10,... | collective-permute-start | bytes 4325384 | tf_op jit(solution)/shard_map/ppermute | solution.py:587
  154.7 19.0 %collective-permute-start.23 = (bf16[2,352,2048]{2,1,0:T(8,128)(2,1)}, bf16[2,352,2048]{2,1,0:T(8,128)(2,1)S(1)}, u32[]{:S(2)}, u32[]{:S(2)}) collective-permute-start(bf16[2,352,2048]{2,1,0:T(8,128)(2,1)} %get-tuple-element.91), channel_id=1, source_target_pairs={{0,1},{1,0},{2,3},{3,2},{4,5},{5,4},{6,7},{7,6},{8,9},{9,8},{10,11... | collective-permute-start | bytes 8650760 | tf_op jit(solution)/shard_map/ppermute | solution.py:587
  (45 other events, 505.7 us)
